TPU v7x, 512 devices: a whole 4x4x16 slice. The times are simulated.
512 devices in a mesh: phi: 64 (over y_lo, z, core), layer: 8 (over y_hi, x).
Axes of the slice: x: 4, y: 4 (y_hi: 2, y_lo: 2; y = y_hi * 2 + y_lo), z: 16, core: 2. Of those that a mesh axis runs over, the one named last changes fastest.
Arguments:
- node_feats: bfloat16 [64, 16384], P(None, ('phi', 'layer')), may hold values from -6 to 6
- edge_feats: bfloat16 [64, 1048576], P(None, ('phi', 'layer')), may hold values from -6 to 6
- edge_source: int32 [1048576], P(('phi', 'layer')), may hold values from 0 to 447
- edge_target: int32 [1048576], P(('phi', 'layer')), may hold values from 0 to 255
- edge_counts: int32 [64, 8], P('phi', 'layer'), may hold values from 256 to 2048, as said below
- rim_upper: int32 [64, 96], P('phi'), may hold values from 0 to 255, as said below
- rim_lower: int32 [64, 96], P('phi'), may hold values from 0 to 255, as said below
- edge_first: bfloat16 [64, 192], replicated, may hold values from -0.4375 to 0.4375
- edge_second: bfloat16 [64, 64], replicated, may hold values from -0.75 to 0.75
- node_first: bfloat16 [64, 128], replicated, may hold values from -0.1875 to 0.1875
- node_second: bfloat16 [64, 64], replicated, may hold values from -0.75 to 0.75
- biases: float32 [4, 64], replicated, may hold values from -3 to 3
- node_cot: float32 [64, 16384], P(None, ('phi', 'layer')), may hold values from -0.5 to 0.5
Outputs:
- node_out: bfloat16 [64, 16384], P(None, ('phi', 'layer'))
- edge_out: bfloat16 [64, 1048576], P(None, ('phi', 'layer'))
- node_grad: float32 [64, 16384], P(None, ('phi', 'layer'))
- grad_edge_first: float32 [64, 192], replicated
- grad_edge_second: float32 [64, 64], replicated
- grad_node_first: float32 [64, 128], replicated
- grad_node_second: float32 [64, 64], replicated
- grad_biases: float32 [4, 64], replicated
Inputs may be any that keep to these rules, and one draw needn't show every extreme that they name: `edge_source`: columns 0 to 255 are the slab's own hits, the next 96 come from the slab below in phi and the last 96 from the slab above, on a closed loop; slots past the count hold any index. `edge_target`: a hit of the edge's own slab. `edge_counts`: slots of a device at or past this count are padding; some device is full in every draw. `rim_upper`: distinct hits of the slab within each row. `rim_lower`: distinct hits of the slab within each row.
All inputs are finite; a program needn't handle non-finite values.
Results may differ from a plain program's by a relative error of at most 0.02.
Values may be sent and summed in bfloat16 or wider, within the bound.
A program may use at most 64 MiB of HBM per device.

v0:
```python
import math

import jax
import jax.numpy as jnp
from jax import lax
from jax.sharding import PartitionSpec as P

ITERS = 2


def from_behind(value, axis, steps):
    count = lax.axis_size(axis)
    pairs = [(source, (source + steps) % count) for source in range(count)]
    return lax.ppermute(value, axis, pairs)


def forward_dot(weight, data):
    return jnp.dot(weight, data, preferred_element_type=jnp.float32)


def back_dot(weight, data):
    return lax.dot_general(
        weight, data, (((0,), (0,)), ((), ())), preferred_element_type=jnp.float32
    )


def exact_back(weight, data):
    return lax.dot_general(
        weight.astype(jnp.float32),
        data,
        (((0,), (0,)), ((), ())),
        precision=lax.Precision.HIGHEST,
        preferred_element_type=jnp.float32,
    )


def outer_dot(left, right):
    return lax.dot_general(
        left, right, (((1,), (1,)), ((), ())), preferred_element_type=jnp.float32
    )


def silu_slope(value):
    logistic = jax.nn.sigmoid(value)
    return logistic * (1.0 + value * (1.0 - logistic))


def column_sums(values, index, width):
    slot_total = values.shape[1]
    block_cols = math.gcd(slot_total, 512)
    block_count = slot_total // block_cols
    positions = jnp.arange(width, dtype=jnp.int32)[:, None]

    def add_block(turn_index, running):
        first_col = turn_index * block_cols
        piece_vals = lax.dynamic_slice_in_dim(values, first_col, block_cols, 1)
        piece_index = lax.dynamic_slice_in_dim(index, first_col, block_cols, 0)
        onehot = (positions == piece_index[None, :]).astype(jnp.bfloat16)
        return running + outer_dot(piece_vals, onehot)

    return lax.fori_loop(
        0, block_count, add_block, jnp.zeros((values.shape[0], width), jnp.float32)
    )


def body(
    node_feats,
    edge_feats,
    edge_source,
    edge_target,
    edge_counts,
    rim_upper,
    rim_lower,
    edge_first,
    edge_second,
    node_first,
    node_second,
    biases,
    node_cot,
):
    latent = node_feats.shape[0]
    groups = lax.axis_size("layer")
    slab_rows = node_feats.shape[1] * groups
    rim_rows = rim_upper.shape[1]
    upper_index = rim_upper[0]
    lower_index = rim_lower[0]
    edge_valid = (jnp.arange(edge_feats.shape[1], dtype=jnp.int32) < edge_counts[0, 0]).astype(
        jnp.float32
    )
    bias_edge = biases[0][:, None]
    bias_message = biases[1][:, None]
    bias_node = biases[2][:, None]
    bias_update = biases[3][:, None]
    first_source = edge_first[:, :latent]
    first_target = edge_first[:, latent : 2 * latent]
    first_self = edge_first[:, 2 * latent :]
    ext_width = slab_rows + 2 * rim_rows
    node_state = node_feats
    edge_state = edge_feats
    stored = []
    for iteration in range(ITERS):
        slab_nodes = lax.all_gather(node_state, "layer", axis=1, tiled=True)
        from_below = from_behind(jnp.take(slab_nodes, upper_index, axis=1), "phi", 1)
        from_above = from_behind(jnp.take(slab_nodes, lower_index, axis=1), "phi", -1)
        slab_nodes, extended = (
            slab_nodes,
            jnp.concatenate([slab_nodes, from_below, from_above], axis=1),
        )
        inputs = jnp.concatenate(
            [
                jnp.take(extended, edge_source, axis=1),
                jnp.take(slab_nodes, edge_target, axis=1),
                edge_state,
            ],
            axis=0,
        )
        hidden_pre = forward_dot(edge_first, inputs) + bias_edge
        hidden = jax.nn.silu(hidden_pre).astype(jnp.bfloat16)
        new_edges = (
            edge_valid
            * (edge_state.astype(jnp.float32) + forward_dot(edge_second, hidden) + bias_message)
        ).astype(jnp.bfloat16)
        partial_value = column_sums(new_edges, edge_target, slab_rows)
        own_messages = lax.psum_scatter(
            partial_value, "layer", scatter_dimension=1, tiled=True
        ).astype(jnp.bfloat16)
        node_in = jnp.concatenate([node_state, own_messages], axis=0)
        node_pre = forward_dot(node_first, node_in) + bias_node
        node_hidden = jax.nn.silu(node_pre).astype(jnp.bfloat16)
        new_nodes = (
            node_state.astype(jnp.float32) + forward_dot(node_second, node_hidden) + bias_update
        ).astype(jnp.bfloat16)
        stored.append((inputs, hidden_pre, hidden, node_in, node_pre, node_hidden))
        node_state = new_nodes
        edge_state = new_edges
    grad_nodes = node_cot
    grad_edges = jnp.zeros(edge_feats.shape, jnp.float32)
    sum_first_edge = jnp.zeros(edge_first.shape, jnp.float32)
    sum_second_edge = jnp.zeros(edge_second.shape, jnp.float32)
    sum_first_node = jnp.zeros(node_first.shape, jnp.float32)
    sum_second_node = jnp.zeros(node_second.shape, jnp.float32)
    edge_bias = jnp.zeros((biases.shape[1],), jnp.float32)
    message_bias = jnp.zeros((biases.shape[1],), jnp.float32)
    node_bias = jnp.zeros((biases.shape[1],), jnp.float32)
    update_bias = jnp.zeros((biases.shape[1],), jnp.float32)
    for iteration in reversed(range(ITERS)):
        inputs, hidden_pre, hidden, node_in, node_pre, node_hidden = stored[iteration]
        nodes_low = grad_nodes.astype(jnp.bfloat16)
        sum_second_node = sum_second_node + outer_dot(nodes_low, node_hidden)
        update_bias = update_bias + jnp.sum(grad_nodes, axis=1)
        node_pre_grad = back_dot(node_second, nodes_low) * silu_slope(node_pre)
        node_pre_low = node_pre_grad.astype(jnp.bfloat16)
        sum_first_node = sum_first_node + outer_dot(node_pre_low, node_in)
        node_bias = node_bias + jnp.sum(node_pre_grad, axis=1)
        node_in_grad = back_dot(node_first, node_pre_low)
        message_grad = node_in_grad[latent:].astype(jnp.bfloat16)
        message_slab = lax.all_gather(message_grad, "layer", axis=1, tiled=True)
        edge_grad = edge_valid * (
            grad_edges + jnp.take(message_slab, edge_target, axis=1).astype(jnp.float32)
        )
        edge_low = edge_grad.astype(jnp.bfloat16)
        sum_second_edge = sum_second_edge + outer_dot(edge_low, hidden)
        message_bias = message_bias + jnp.sum(edge_grad, axis=1)
        pre_grad = back_dot(edge_second, edge_low) * silu_slope(hidden_pre)
        pre_low = pre_grad.astype(jnp.bfloat16)
        sum_first_edge = sum_first_edge + outer_dot(pre_low, inputs)
        edge_bias = edge_bias + jnp.sum(pre_grad, axis=1)
        grad_edges = edge_grad + back_dot(first_self, pre_low)
        source_pre = column_sums(pre_low, edge_source, ext_width)
        target_pre = column_sums(pre_low, edge_target, slab_rows)
        extended_grad = exact_back(first_source, source_pre)
        slab_grad = extended_grad[:, :slab_rows] + exact_back(first_target, target_pre)
        upper_grad = extended_grad[:, slab_rows : slab_rows + rim_rows]
        lower_grad = extended_grad[:, slab_rows + rim_rows :]
        upper_back = from_behind(upper_grad, "phi", -1)
        lower_back = from_behind(lower_grad, "phi", 1)
        slab_grad = slab_grad.at[:, upper_index].add(upper_back).at[:, lower_index].add(lower_back)
        own_grad = lax.psum_scatter(
            slab_grad.astype(jnp.bfloat16), "layer", scatter_dimension=1, tiled=True
        ).astype(jnp.float32)
        grad_nodes = grad_nodes + node_in_grad[:latent] + own_grad
    totals = lax.psum(
        (
            sum_first_edge,
            sum_second_edge,
            sum_first_node,
            sum_second_node,
            jnp.stack([edge_bias, message_bias, node_bias, update_bias]),
        ),
        ("phi", "layer"),
    )
    return (
        node_state,
        edge_state,
        grad_nodes,
        totals[0],
        totals[1],
        totals[2],
        totals[3],
        totals[4],
    )


def solution(mesh):
    return jax.shard_map(
        body,
        mesh=mesh,
        in_specs=(
            P(None, ("phi", "layer")),
            P(None, ("phi", "layer")),
            P(("phi", "layer")),
            P(("phi", "layer")),
            P("phi", "layer"),
            P("phi", None),
            P("phi", None),
            P(),
            P(),
            P(),
            P(),
            P(),
            P(None, ("phi", "layer")),
        ),
        out_specs=(
            P(None, ("phi", "layer")),
            P(None, ("phi", "layer")),
            P(None, ("phi", "layer")),
            P(),
            P(),
            P(),
            P(),
            P(),
        ),
        check_vma=False,
    )
```

profile of v0, /device:TPU:1, one launch (start us, length us, event | category | flops | bytes accessed | tf_op | source)
XLA Modules:
  0.0 1056.2 jit_solution(11095163154803151010)
XLA Ops:
  8.6 29.6 %all_gather.12 = bf16[64,256]{0,1:T(8,128)(2,1)S(1)} all-gather(bf16[64,32]{0,1:T(8,128)(2,1)} %param.31), channel_id=1, replica_groups=mesh['phi'=64,'layer'=8] {'layer'}, dimensions={1}, use_global_device_ids=true | all-gather | bytes 36864 | tf_op jit(solution)/shard_map/all_gather | solution.py:102
  38.9 10.3 collective-permute-start
  51.3 5.2 collective-permute-start.1
  58.7 6.2 gather_fusion.3
  66.8 6.2 gather_fusion.2
  75.3 1.4 while.84
  76.7 0.8 copy.82
  77.5 84.4 %reduce-scatter.13.cloned.1.call-done = f32[32,64]{1,0:T(8,128)} async-done(((f32[256,64]{1,0:T(8,128)}), f32[32,64]{1,0:T(8,128)}) %reduce-scatter.13.cloned.1.call-update) | async-done | bytes 8208
  163.0 27.8 %all_gather.13 = bf16[64,256]{0,1:T(8,128)(2,1)S(1)} all-gather(bf16[64,32]{0,1:T(8,128)(2,1)S(1)} %fusion.54), channel_id=1, replica_groups=mesh['phi'=64,'layer'=8] {'layer'}, dimensions={1}, use_global_device_ids=true | all-gather | bytes 36864 | tf_op jit(solution)/shard_map/all_gather | solution.py:102
  192.2 12.0 %collective-permute-start.2 = (bf16[64,96]{0,1:T(8,128)(2,1)S(1)}, bf16[64,96]{0,1:T(8,128)(2,1)S(1)}, u32[]{:S(2)}, u32[]{:S(2)}) collective-permute-start(bf16[64,96]{0,1:T(8,128)(2,1)S(1)} %select_bitcast_fusion.5), channel_id=1, source_target_pairs={{0,8},{8,16},{16,24},{24,32},{32,40},{40,48},{48,56},{56,64},{64,7... | collective-permute-start | bytes 36872 | tf_op jit(solution)/shard_map/ppermute | solution.py:14
  204.3 1.9 collective-permute-start.3
  206.3 6.2 gather_fusion.7
  212.8 6.2 gather_fusion.6
  219.2 1.1 multiply_convert_fusion
  221.2 1.4 while.85
  222.6 0.8 copy.70
  223.4 83.3 %reduce-scatter.7.cloned.1.call-done = f32[64,32]{0,1:T(8,128)} async-done(((f32[64,256]{0,1:T(8,128)}), f32[64,32]{0,1:T(8,128)}) %reduce-scatter.7.cloned.1.call-update) | async-done | bytes 8208 | tf_op jit(solution)/shard_map/reduce_scatter | solution.py:124
  308.2 27.8 %all_gather.14 = bf16[64,256]{0,1:T(8,128)(2,1)S(1)} all-gather(bf16[64,32]{0,1:T(8,128)(2,1)S(1)} %slice.125), channel_id=1, replica_groups=mesh['phi'=64,'layer'=8] {'layer'}, dimensions={1}, use_global_device_ids=true | all-gather | bytes 36864 | tf_op jit(solution)/shard_map/all_gather | solution.py:157
  336.0 6.2 gather_fusion.8
  342.6 0.8 copy-done.30
  344.3 1.7 while.86
  346.3 1.4 while.87
  348.7 10.8 %collective-permute-start.4 = (f32[64,96]{1,0:T(8,128)S(1)}, f32[64,96]{1,0:T(8,128)S(1)}, u32[]{:S(2)}, u32[]{:S(2)}) collective-permute-start(f32[64,96]{1,0:T(8,128)S(1)} %get-tuple-element.777), channel_id=1, source_target_pairs={{0,504},{8,0},{16,8},{24,16},{32,24},{40,32},{48,40},{56,48},{64,5... | collective-permute-start | bytes 73736 | tf_op jit(solution)/shard_map/ppermute | solution.py:14
  359.5 3.1 collective-permute-start.5
  363.7 1.2 scatter_fusion
  364.9 1.2 scatter_fusion.1
  366.9 83.6 %reduce-scatter.9.cloned.1.call-done = bf16[64,32]{0,1:T(8,128)(2,1)} async-done(((bf16[64,256]{0,1:T(8,128)(2,1)}), bf16[64,32]{0,1:T(8,128)(2,1)}) %reduce-scatter.9.cloned.1.call-update) | async-done | bytes 4112 | tf_op jit(solution)/shard_map/reduce_scatter | solution.py:178
  451.6 27.8 %all_gather.15 = bf16[64,256]{0,1:T(8,128)(2,1)S(1)} all-gather(bf16[64,32]{0,1:T(8,128)(2,1)S(1)} %slice.124), channel_id=1, replica_groups=mesh['phi'=64,'layer'=8] {'layer'}, dimensions={1}, use_global_device_ids=true | all-gather | bytes 36864 | tf_op jit(solution)/shard_map/all_gather | solution.py:157
  479.4 6.2 gather_fusion.9
  485.8 1.4 fusion.105
  487.7 0.8 convolution_add_fusion.9
  488.5 0.8 convolution_add_fusion.10
  489.3 0.9 convolution_add_fusion.11
  491.3 1.0 convolution_add_fusion.8
  492.4 1.7 while.88
  494.3 1.4 while.89
  495.8 10.8 %collective-permute-start.6 = (f32[64,96]{1,0:T(8,128)S(1)}, f32[64,96]{1,0:T(8,128)S(1)}, u32[]{:S(2)}, u32[]{:S(2)}) collective-permute-start(f32[64,96]{1,0:T(8,128)S(1)} %get-tuple-element.775), channel_id=1, source_target_pairs={{0,504},{8,0},{16,8},{24,16},{32,24},{40,32},{48,40},{56,48},{64,5... | collective-permute-start | bytes 73736 | tf_op jit(solution)/shard_map/ppermute | solution.py:14
  506.6 3.1 collective-permute-start.7
  511.0 1.2 scatter_fusion.2
  512.2 1.2 scatter_fusion.3
  514.8 447.0 %all-reduce.3.cloned.1.call-done = (f32[64,192]{1,0:T(8,128)}, f32[64,64]{1,0:T(8,128)}, f32[64,128]{1,0:T(8,128)}, f32[64,64]{0,1:T(8,128)}, f32[4,64]{1,0:T(4,128)}) async-done(((f32[64,192]{1,0:T(8,128)}, f32[64,64]{1,0:T(8,128)}, f32[64,128]{1,0:T(8,128)}, f32[64,64]{0,1:T(8,128)}, f32[4,64]{1,0:T(4,128)}), (f32[64,192]{1,0:T(8,128)}, f32[64,64]{1,0:T(8,128)}, f32[64,128]{1,0:T(8,128)}, ...) | async-done | bytes 115728 | tf_op jit(solution)/shard_map/psum | solution.py:182
  961.7 1.5 copy.80
  963.2 79.7 %reduce-scatter.11.cloned.1.call-done = bf16[64,32]{0,1:T(8,128)(2,1)} async-done(((bf16[64,256]{0,1:T(8,128)(2,1)}), bf16[64,32]{0,1:T(8,128)(2,1)}) %reduce-scatter.11.cloned.1.call-update) | async-done | bytes 4112 | tf_op jit(solution)/shard_map/reduce_scatter | solution.py:178
  1042.9 1.3 fusion.66
  1044.2 1.5 copy.130
  1045.6 1.4 copy.131
  1047.0 1.4 copy.132
  1048.4 1.2 copy.133
  (207 shorter events, 33.9 us)
Async XLA Ops:
  7.2 67.3 %copy-start = (bf16[64,64]{1,0:T(8,128)(2,1)S(1)}, bf16[64,64]{1,0:T(8,128)(2,1)}, u32[]{:S(2)}) copy-start(bf16[64,64]{1,0:T(8,128)(2,1)} %param.39) | copy-start | bytes 24580
  7.2 51.5 %copy-start.1 = (s32[2048]{0:T(1024)S(1)}, s32[2048]{0:T(1024)}, u32[]{:S(2)}) copy-start(s32[2048]{0:T(1024)} %param.34) | copy-start | bytes 24580
  7.2 154.7 %reduce-scatter.13.cloned.1.call-start = ((), (), s32[]{:S(2)}) async-start(), calls=%async_computation.7 | async-start | bytes 147456
  38.9 27.8 %collective-permute-start = (bf16[64,96]{0,1:T(8,128)(2,1)S(1)}, bf16[64,96]{0,1:T(8,128)(2,1)S(1)}, u32[]{:S(2)}, u32[]{:S(2)}) collective-permute-start(bf16[64,96]{0,1:T(8,128)(2,1)S(1)} %select_bitcast_fusion.7), channel_id=1, source_target_pairs={{0,8},{8,16},{16,24},{24,32},{32,40},{40,48},{48,56},{56,64},{64,7... | collective-permute-start | bytes 36872 | tf_op jit(solution)/shard_map/ppermute | solution.py:14
  51.3 15.4 %collective-permute-start.1 = (bf16[64,96]{0,1:T(8,128)(2,1)S(1)}, bf16[64,96]{0,1:T(8,128)(2,1)S(1)}, u32[]{:S(2)}, u32[]{:S(2)}) collective-permute-start(bf16[64,96]{0,1:T(8,128)(2,1)S(1)} %select_bitcast_fusion.6), channel_id=1, source_target_pairs={{0,504},{8,0},{16,8},{24,16},{32,24},{40,32},{48,40},{56,48},{64,5... | collective-permute-start | bytes 36872 | tf_op jit(solution)/shard_map/ppermute | solution.py:14
  58.6 6.2 copy-start.22
  65.5 1.0 copy-start.2
  73.0 0.8 copy-start.11
  74.4 0.8 copy-start.28
  75.3 87.4 %copy-start.3 = (bf16[64,128]{1,0:T(8,128)(2,1)S(1)}, bf16[64,128]{1,0:T(8,128)(2,1)}, u32[]{:S(2)}) copy-start(bf16[64,128]{1,0:T(8,128)(2,1)} %param.40) | copy-start | bytes 49156
  75.3 87.4 %copy-start.12 = (bf16[64,32]{0,1:T(8,128)(2,1)S(1)}, bf16[64,32]{0,1:T(8,128)(2,1)}, u32[]{:S(2)}) copy-start(bf16[64,32]{0,1:T(8,128)(2,1)} %param.31) | copy-start | bytes 12292
  75.3 87.6 %copy-start.23 = (bf16[64,64]{1,0:T(8,128)(2,1)S(1)}, bf16[64,64]{1,0:T(8,128)(2,1)}, u32[]{:S(2)}) copy-start(bf16[64,64]{1,0:T(8,128)(2,1)} %param.41) | copy-start | bytes 24580
  76.6 129.6 %copy-start.24 = (s32[1,96]{1,0:T(1,128)S(1)}, s32[1,96]{1,0:T(1,128)}, u32[]{:S(2)}) copy-start(s32[1,96]{1,0:T(1,128)} %param.36) | copy-start | bytes 1156
  77.4 229.3 %reduce-scatter.7.cloned.1.call-start = ((), (), s32[]{:S(2)}) async-start(), calls=%async_computation.4 | async-start | bytes 147456 | tf_op jit(solution)/shard_map/reduce_scatter | solution.py:124
  162.6 43.6 %copy-start.14 = (bf16[64,32]{0,1:T(8,128)(2,1)}, bf16[64,32]{0,1:T(8,128)(2,1)S(1)}, u32[]{:S(2)}) copy-start(bf16[64,32]{0,1:T(8,128)(2,1)S(1)} %bitcast_convert_fusion) | copy-start | bytes 12292
  162.8 27.9 %copy-start.19 = (f32[64,32]{0,1:T(8,128)}, f32[64,32]{0,1:T(8,128)S(1)}, u32[]{:S(2)}) copy-start(f32[64,32]{0,1:T(8,128)S(1)} %fusion.53) | copy-start | bytes 24580
  192.2 20.5 %collective-permute-start.2 = (bf16[64,96]{0,1:T(8,128)(2,1)S(1)}, bf16[64,96]{0,1:T(8,128)(2,1)S(1)}, u32[]{:S(2)}, u32[]{:S(2)}) collective-permute-start(bf16[64,96]{0,1:T(8,128)(2,1)S(1)} %select_bitcast_fusion.5), channel_id=1, source_target_pairs={{0,8},{8,16},{16,24},{24,32},{32,40},{40,48},{48,56},{56,64},{64,7... | collective-permute-start | bytes 36872 | tf_op jit(solution)/shard_map/ppermute | solution.py:14
  204.3 8.4 collective-permute-start.3
  219.2 1.1 copy-start.5
  219.2 1.1 copy-start.7
  220.3 0.8 copy-start.16
  221.2 2.2 copy-start.25
  221.2 86.5 %copy-start.21 = (f32[64,32]{0,1:T(8,128)S(1)}, f32[64,32]{0,1:T(8,128)}, u32[]{:S(2)}) copy-start(f32[64,32]{0,1:T(8,128)} %param.43) | copy-start | bytes 24580
  222.5 119.6 %copy-start.4 = (bf16[64,2048]{1,0:T(8,128)(2,1)}, bf16[64,2048]{1,0:T(8,128)(2,1)S(1)}, u32[]{:S(2)}) copy-start(bf16[64,2048]{1,0:T(8,128)(2,1)S(1)} %get-tuple-element.1128) | copy-start | bytes 786436
  223.4 227.2 %reduce-scatter.9.cloned.1.call-start = ((), (), s32[]{:S(2)}) async-start(), calls=%async_computation.5 | async-start | bytes 73728 | tf_op jit(solution)/shard_map/reduce_scatter | solution.py:178
  342.4 1.0 copy-start.30
  343.4 0.7 copy-start.9
  343.4 0.9 copy-start.10
  344.3 2.0 copy-start.18
  347.7 0.7 copy-start.26
  348.7 14.2 %collective-permute-start.4 = (f32[64,96]{1,0:T(8,128)S(1)}, f32[64,96]{1,0:T(8,128)S(1)}, u32[]{:S(2)}, u32[]{:S(2)}) collective-permute-start(f32[64,96]{1,0:T(8,128)S(1)} %get-tuple-element.777), channel_id=1, source_target_pairs={{0,504},{8,0},{16,8},{24,16},{32,24},{40,32},{48,40},{56,48},{64,5... | collective-permute-start | bytes 73736 | tf_op jit(solution)/shard_map/ppermute | solution.py:14
  359.5 4.1 collective-permute-start.5
  364.9 86.4 %copy-start.20 = (f32[64,32]{0,1:T(8,128)S(1)}, f32[64,32]{0,1:T(8,128)}, u32[]{:S(2)}) copy-start(f32[64,32]{0,1:T(8,128)} %copy-done.19) | copy-start | bytes 24580
  366.7 595.0 %all-reduce.3.cloned.1.call-start = ((), (), s32[]{:S(2)}) async-start(), calls=%async_computation.8 | async-start | bytes 331776 | tf_op jit(solution)/shard_map/psum | solution.py:182
  485.8 1.4 copy-start.29
  487.2 1.3 copy-start.13
  487.2 1.3 copy-start.15
  490.2 0.9 copy-start.6
  490.2 1.0 copy-start.8
  490.2 1.1 copy-start.27
  492.4 2.0 copy-start.17
  495.8 15.1 %collective-permute-start.6 = (f32[64,96]{1,0:T(8,128)S(1)}, f32[64,96]{1,0:T(8,128)S(1)}, u32[]{:S(2)}, u32[]{:S(2)}) collective-permute-start(f32[64,96]{1,0:T(8,128)S(1)} %get-tuple-element.775), channel_id=1, source_target_pairs={{0,504},{8,0},{16,8},{24,16},{32,24},{40,32},{48,40},{56,48},{64,5... | collective-permute-start | bytes 73736 | tf_op jit(solution)/shard_map/ppermute | solution.py:14
  506.6 4.3 collective-permute-start.7
  510.4 532.5 %reduce-scatter.11.cloned.1.call-start = ((), (), s32[]{:S(2)}) async-start(), calls=%async_computation.6 | async-start | bytes 73728 | tf_op jit(solution)/shard_map/reduce_scatter | solution.py:178
Sparse Core Ops, SparseCore 0:
  77.6 84.3 reduce-scatter.12
  223.5 83.1 reduce-scatter.6
  366.8 83.6 reduce-scatter.8
  510.5 451.1 all-reduce.2
  967.2 75.5 reduce-scatter.10
where the time goes:
time: 1060 us
  waiting for transfers between devices  779 us (73%)
  blocking collectives  113 us (11%)
  starting transfers between devices  57.4 us (5%)
  local copies, waits for them, and re-layouts  56.5 us (5%)
  matrix products  18.7 us (2%)
  other arithmetic  16 us (2%)
  between operations  15.2 us (1%)
    psum x1, waiting for transfers between devices, body(): lax.psum((sum_first_edge, sum_second_edge, sum_first_node, sum_second_nod...  447 us
    reduce_scatter x2, waiting for transfers between devices, body(): lax.psum_scatter(slab_grad.astype(jnp.bfloat16), 'layer', scatter_dimensi...  163 us
    unnamed x6, waiting for transfers between devices  84.5 us
    reduce_scatter x1, waiting for transfers between devices, body(): lax.psum_scatter(partial_value, 'layer', scatter_dimension=1, tiled=True)  83.3 us
    all_gather x2, blocking collectives, body(): slab_nodes = lax.all_gather(node_state, 'layer', axis=1, tiled=True)  57.4 us
    ppermute x8, starting transfers between devices, from_behind(): return lax.ppermute(value, axis, pairs)  57.2 us
    all_gather x2, blocking collectives, body(): message_slab = lax.all_gather(message_grad, 'layer', axis=1, tiled=True)  55.6 us
  transfers between devices with their start and end apart: 13, of which 6 were waited for; matrix products, arithmetic and copies ran while one was open for 2% of the time, Pallas kernels for 0%

commit v1 on v0

v1 whole, which is shorter than its diff:
```python
import functools
import itertools

import jax
import jax.numpy as jnp
from jax import lax
from jax.experimental import pallas as pl
from jax.experimental.pallas import tpu as pltpu
from jax.sharding import PartitionSpec as P

MESH = pl.DeviceIdType.MESH
BF16 = jnp.bfloat16
F32 = jnp.float32
LANES = 128
Y_LO = 2
CORES = 2
CHUNK = 512


def nn(left, right):
    return lax.dot_general(left, right, (((1,), (0,)), ((), ())), preferred_element_type=F32)


def nt(left, right):
    return lax.dot_general(left, right, (((1,), (1,)), ((), ())), preferred_element_type=F32)


def nt_exact(left, right):
    return lax.dot_general(
        left,
        right,
        (((1,), (1,)), ((), ())),
        precision=lax.Precision.HIGHEST,
        preferred_element_type=F32,
    )


def pick(rows, cols, row_shift, col_limit, dtype=BF16):
    row = lax.broadcasted_iota(jnp.int32, (rows, cols), 0)
    col = lax.broadcasted_iota(jnp.int32, (rows, cols), 1)
    return jnp.where((row == col + row_shift) & (col < col_limit), 1.0, 0.0).astype(dtype)


def two_parts(value):
    main = value.astype(BF16)
    return jnp.concatenate([main, (value - main.astype(F32)).astype(BF16)], axis=0)


def logistic(value):
    return 0.5 * jnp.tanh(0.5 * value) + 0.5


def chunks(total, step):
    size = min(CHUNK, total)

    def run(turn, carry):
        step(pl.ds(pl.multiple_of(turn * size, size), size))
        return carry

    lax.fori_loop(0, total // size, run, 0, unroll=True)


def wait_bytes(ref, sem):
    pltpu.make_async_copy(ref, ref, sem).wait()


def far_first(sizes):
    steps = list(itertools.product(*(range(size) for size in sizes)))
    hops = lambda step: sum(min(at, size - at) for at, size in zip(step, sizes))
    return sorted(steps[1:], key=hops, reverse=True)


def kernel(
    n_phi,
    n_layer,
    feats_in,
    edges_in,
    source_in,
    target_in,
    count_in,
    rim_up_in,
    rim_down_in,
    first_in,
    second_in,
    node_first_in,
    node_second_in,
    biases_in,
    cot_in,
    node_out,
    edge_out,
    node_grad,
    grad_first,
    grad_second,
    grad_node_first,
    grad_node_second,
    grad_biases,
    feats,
    edges0,
    source,
    target,
    count,
    rim_up,
    rim_down,
    first,
    second,
    node_first,
    node_second,
    biases,
    cot,
    onehot,
    rim_pick,
    rim_put,
    hidden_in,
    edge_new,
    z_part,
    slopes,
    grad_edge,
    second_grad_edge,
    back_stack,
    node_kept,
    grad_kept,
    own_send,
    slab_land,
    rim_send,
    rim_land,
    message_land,
    swap_land,
    back_send,
    back_land,
    comb_send,
    comb_land,
    grads,
    plane_land,
    z_land,
    grads_sum,
    load_sem,
    send_sem,
    recv_sem,
):
    hits, latent = feats.shape
    slots = edges0.shape[1]
    slab = hits * n_layer
    half = slab // 2
    rim = rim_up.shape[1]
    n_z = n_phi // (Y_LO * CORES)
    n_plane = Y_LO * CORES * n_layer
    n_x = n_layer // 2
    n_y = 2 * Y_LO
    shard = grads.shape[0] // n_plane
    phi = lax.axis_index("phi")
    layer = lax.axis_index("layer")
    core = lax.rem(phi, CORES)
    z_at = lax.rem(lax.div(phi, CORES), n_z)
    y_lo = lax.div(phi, CORES * n_z)
    y_hi = lax.div(layer, n_x)
    x_at = lax.rem(layer, n_x)
    y_at = y_hi * Y_LO + y_lo
    plane_at = (y_lo * CORES + core) * n_layer + layer
    above = lax.rem(phi + 1, n_phi)
    below = lax.rem(phi + n_phi - 1, n_phi)

    x_of = [lax.rem(x_at + step, n_x) for step in range(n_x)]
    y_hi_of = [lax.rem(y_hi + step, 2) * n_x for step in range(2)]
    layer_peers = [
        y_hi_of[dy // Y_LO] + x_of[dx]
        for dy, dx in far_first((n_y, n_x))
        if dy % Y_LO == 0
    ]
    y_of = [lax.rem(y_at + step, n_y) for step in range(n_y)]
    pair_of = [lax.rem(y, Y_LO) * CORES for y in y_of]
    phi_base = [lax.rem(y, Y_LO) * (CORES * n_z) + z_at * CORES for y in y_of]
    layer_base = [lax.div(y, Y_LO) * n_x for y in y_of]
    core_of = [core, 1 - core]
    plane_peers = []
    for dy, dx, dc in far_first((n_y, n_x, CORES)):
        device = (phi_base[dy] + core_of[dc], layer_base[dy] + x_of[dx])
        plane_peers.append((device, (pair_of[dy] + core_of[dc]) * n_layer + device[1]))
    z_peers = [
        (y_lo * (CORES * n_z) + lax.rem(z_at + step, n_z) * CORES + core, layer)
        for (step,) in far_first((n_z,))
    ]

    def send(src, dst, step, device):
        pltpu.make_async_remote_copy(
            src_ref=src,
            dst_ref=dst,
            send_sem=send_sem.at[step],
            recv_sem=recv_sem.at[step],
            device_id=device,
            device_id_type=MESH,
        ).start()

    barrier = pltpu.get_barrier_semaphore()
    greeted = z_peers + [device for device, _ in plane_peers] + [(above, layer), (below, layer)]
    for device in greeted:
        pl.semaphore_signal(barrier, inc=1, device_id=device, device_id_type=MESH)

    loads = [
        pltpu.make_async_copy(src, dst, load_sem.at[at])
        for at, (src, dst) in enumerate(
            (
                (feats_in, feats),
                (cot_in, cot),
                (first_in, first),
                (biases_in, biases),
                (second_in, second),
                (node_first_in, node_first),
                (node_second_in, node_second),
                (count_in, count),
                (source_in, source),
                (target_in, target),
                (rim_up_in, rim_up),
                (rim_down_in, rim_down),
                (edges_in, edges0),
            )
        )
    ]
    for load in loads:
        load.start()

    lane = lax.broadcasted_iota(jnp.int32, (1, LANES), 1)
    low_half = lane < latent
    own_rows = pl.ds(pl.multiple_of(layer * hits, hits), hits)
    swap_rows = pl.ds(pl.multiple_of(layer * half, half), half)

    loads[0].wait()
    loads[1].wait()
    wide_pick = pick(latent, LANES, 0, latent)
    high_pick = pick(latent, LANES, -latent, LANES)
    own_send[...] = (
        nn(feats[...], wide_pick) + nn(cot[...].astype(BF16), high_pick)
    ).astype(BF16)
    pl.semaphore_wait(barrier, len(greeted))
    for peer in layer_peers:
        send(own_send, slab_land.at[own_rows, :], 0, (phi, peer))
    slab_land[own_rows, :] = own_send[...]

    swaps = (message_land, swap_land.at[0], swap_land.at[1])

    def swap(at, value):
        swaps[at][swap_rows, :] = value.astype(swaps[at].dtype)
        mine = swaps[at].at[swap_rows, :]
        for peer in layer_peers:
            send(mine, mine, 3 + at, (phi, peer))

    def swapped_sum(at):
        wait_bytes(swaps[at].at[pl.ds(0, (n_layer - 1) * half), :], recv_sem.at[3 + at])
        total = swaps[at][0:half, :].astype(F32)
        for turn in range(1, n_layer):
            total = total + swaps[at][turn * half : (turn + 1) * half, :].astype(F32)
        return total

    for load in loads[2:7]:
        load.wait()
    edge_first = first[...]
    source_wide = nn(edge_first, pick(3 * latent, LANES, 0, latent)).astype(BF16)
    target_wide = nn(edge_first, pick(3 * latent, LANES, latent, latent)).astype(BF16)
    source_high = nn(edge_first, pick(3 * latent, LANES, -latent, LANES) * (~low_half).astype(BF16)).astype(BF16)
    target_high = nn(edge_first, pick(3 * latent, LANES, 0, LANES) * (~low_half).astype(BF16)).astype(BF16)
    first_self = edge_first[:, 2 * latent :]
    edge_second = second[...]
    square_eye = pick(latent, latent, 0, latent)
    self_back = nt(square_eye, first_self).astype(BF16)
    second_back = nt(square_eye, edge_second).astype(BF16)
    zero_square = jnp.zeros((latent, latent), BF16)
    gm_pick = jnp.concatenate(
        [
            high_pick,
            nt(square_eye, jnp.concatenate([zero_square, edge_second], axis=0)).astype(BF16),
        ],
        axis=0,
    )
    first_back = jnp.concatenate([source_wide, target_wide], axis=0)
    first_back_high = jnp.concatenate([source_high, target_high], axis=0)
    node_first_wide = jnp.concatenate(
        [node_first[...], jnp.zeros((LANES - latent, 2 * latent), BF16)], axis=0
    )
    node_second_low = nn(node_second[...], wide_pick).astype(BF16)
    zero_wide = jnp.zeros((LANES - latent, LANES), BF16)
    node_second_wide = jnp.concatenate([node_second_low, zero_wide], axis=0)
    node_second_under = jnp.concatenate([zero_wide, node_second_low], axis=0)
    bias_rows = lax.dot_general(
        biases[...],
        pick(latent, LANES, 0, latent, F32),
        (((1,), (0,)), ((), ())),
        precision=lax.Precision.HIGHEST,
        preferred_element_type=F32,
    )
    bias_cols = nt_exact(pick(latent, latent, 0, latent, F32), biases[...])
    bias_edge = bias_cols[:, 0:1]
    bias_message = bias_cols[:, 1:2]
    bias_node = bias_rows[2:3, :]
    bias_update = bias_rows[3:4, :]
    for load in loads[7:]:
        load.wait()

    def build(cols):
        width = cols.size
        spot = lax.broadcasted_iota(jnp.int32, (1, width), 1) + cols.start
        here = spot < count[...]
        source_at = jnp.where(here, source[:, cols], -1)
        target_at = jnp.where(here, target[:, cols], -1)
        row = lax.broadcasted_iota(jnp.int32, (slab, width), 0)
        onehot[0:slab, cols] = jnp.where(row == source_at, 1.0, 0.0).astype(BF16)
        onehot[slab : 2 * slab, cols] = jnp.where(row == target_at, 1.0, 0.0).astype(BF16)
        rim_row = lax.broadcasted_iota(jnp.int32, (2 * rim, width), 0) + slab
        onehot[2 * slab : 2 * slab + 2 * rim, cols] = jnp.where(
            rim_row == source_at, 1.0, 0.0
        ).astype(BF16)
        z_part[:, cols] = nn(first_self, edges0[:, cols]) + bias_edge

    chunks(slots, build)
    rim_eye = pick(rim, rim, 0, rim)
    for side, index in enumerate((rim_up, rim_down)):
        put = jnp.where(
            lax.broadcasted_iota(jnp.int32, (slab, rim), 0) == index[...], 1.0, 0.0
        ).astype(BF16)
        rim_put[side] = put
        rim_pick[side * rim : (side + 1) * rim, :] = nt(rim_eye, put).astype(BF16)
    grad_own = lax.dot_general(
        cot[...],
        pick(latent, LANES, 0, latent, F32),
        (((1,), (0,)), ((), ())),
        precision=lax.Precision.HIGHEST,
        preferred_element_type=F32,
    )

    wait_bytes(slab_land.at[pl.ds(0, slab - hits), :], recv_sem.at[0])
    table = jnp.where(low_half, slab_land[...].astype(F32), 0.0).astype(BF16)
    for k in range(2):
        rim_send[k] = nn(rim_pick[...], table).astype(BF16)
        send(rim_send.at[k, 0:rim], rim_land.at[k, 0:rim], 1 + k, (above, layer))
        send(
            rim_send.at[k, rim : 2 * rim],
            rim_land.at[k, rim : 2 * rim],
            1 + k,
            (below, layer),
        )
        own_part = two_parts(
            jnp.concatenate([nt(source_wide, table), nt(target_wide, table)], axis=1)
        )

        def own_terms(cols):
            terms = nn(own_part, onehot[0 : 2 * slab, cols])
            z_part[:, cols] = z_part[:, cols] + (terms[0:latent] + terms[latent:])

        chunks(slots, own_terms)
        wait_bytes(rim_land.at[k], recv_sem.at[1 + k])
        rim_part = two_parts(nt(source_wide, rim_land[k]))

        def edge_mlp(cols):
            width = cols.size
            terms = nn(rim_part, onehot[2 * slab : 2 * slab + 2 * rim, cols])
            pre = z_part[:, cols] + (terms[0:latent] + terms[latent:])
            gate = logistic(pre)
            hidden = (pre * gate).astype(BF16)
            hidden_in[k, 3 * latent : 4 * latent, cols] = hidden
            slopes[k, :, cols] = gate * (1.0 + pre * (1.0 - gate))
            old = edges0[:, cols] if k == 0 else edge_new[0, 0:latent, cols]
            here = lax.broadcasted_iota(jnp.int32, (1, width), 1) + cols.start < count[...]
            fresh = jnp.where(
                here, old.astype(F32) + nn(edge_second, hidden) + bias_message, 0.0
            ).astype(BF16)
            edge_new[k, 0:latent, cols] = fresh
            edge_new[k, latent : 2 * latent, cols] = fresh

        chunks(slots, edge_mlp)
        both_halves = nt(onehot[slab : 2 * slab, :], edge_new[k])
        swap(k, jnp.where(low_half, both_halves[0:half], both_halves[half:]))

        raw_own = nt(wide_pick, table).astype(BF16)
        raw_rim = nt(wide_pick, rim_land[k]).astype(BF16)

        def inputs(cols):
            hidden_in[k, 0:latent, cols] = (
                nn(raw_own, onehot[0:slab, cols])
                + nn(raw_rim, onehot[2 * slab : 2 * slab + 2 * rim, cols])
            ).astype(BF16)
            hidden_in[k, latent : 2 * latent, cols] = nn(
                raw_own, onehot[slab : 2 * slab, cols]
            ).astype(BF16)
            if k == 0:
                old = edges0[:, cols]
                z_part[:, cols] = nn(first_self, edge_new[0, 0:latent, cols]) + bias_edge
            else:
                old = edge_new[0, 0:latent, cols]
                edge_out[:, cols] = edge_new[1, 0:latent, cols]
            hidden_in[k, 2 * latent : 3 * latent, cols] = old

        chunks(slots, inputs)
        packed = swapped_sum(k)
        turned = pltpu.roll(packed, latent, 1)
        table_wide = table.astype(F32)
        node_in = jnp.concatenate(
            [
                jnp.where(low_half, table_wide[0:half], turned),
                jnp.where(low_half, table_wide[half:], packed),
            ],
            axis=0,
        ).astype(BF16)
        node_pre = nt(node_in, node_first_wide) + bias_node
        node_gate = logistic(node_pre)
        node_hidden = (node_pre * node_gate).astype(BF16)
        node_slope = node_gate * (1.0 + node_pre * (1.0 - node_gate))
        node_kept[k, 0] = node_in
        node_kept[k, 1] = node_hidden
        if k == 0:
            first_slope = node_slope
        table = (table_wide + nt(node_hidden, node_second_wide) + bias_update).astype(BF16)

    for k in (1, 0):
        if k == 1:
            pre_back = nn(slab_land[...], node_second_under) * node_slope
        else:
            grad_low = grad_now.astype(BF16)
            pre_back = nn(grad_low, node_second_wide) * first_slope
        pre_low = pre_back.astype(BF16)
        in_back = nn(pre_low, node_first_wide)
        gm_part = nt(gm_pick, in_back.astype(BF16))
        gm_part = jnp.concatenate([gm_part[0:latent].astype(BF16), two_parts(gm_part[latent:])], axis=0)

        def edge_back(cols):
            both = nn(gm_part, onehot[slab : 2 * slab, cols])
            edge_grad = both[0:latent]
            hidden_grad = both[latent : 2 * latent] + both[2 * latent :]
            if k == 0:
                edge_grad = edge_grad + grad_edge[:, cols]
                hidden_grad = hidden_grad + second_grad_edge[:, cols]
            else:
                grad_edge[:, cols] = edge_grad
            pre_grad = (hidden_grad * slopes[k, :, cols]).astype(BF16)
            back_stack[0:latent, cols] = pre_grad
            back_stack[latent : 2 * latent, cols] = pre_grad
            back_stack[2 * latent : 3 * latent, cols] = edge_grad.astype(BF16)

        chunks(slots, edge_back)

        def weight_terms():
            outer = nt(back_stack[latent : 3 * latent, :], hidden_in[k])
            upper = outer[0:latent, 0:LANES]
            lower = jnp.where(low_half, outer[0:latent, LANES:], outer[latent:, LANES:])
            ones = jnp.ones((8, slots), BF16)
            pre_sums = nt(ones, back_stack[0 : 2 * latent, :])
            edge_sums = nt(ones, back_stack[latent : 3 * latent, :])
            row = lax.broadcasted_iota(jnp.int32, (8, LANES), 0)
            bias_terms = jnp.where(
                low_half,
                0.0,
                jnp.where(row == 0, pre_sums, jnp.where(row == 1, edge_sums, 0.0)),
            )
            return upper, lower, bias_terms

        if k == 0:
            upper, lower, bias_terms = weight_terms()
            grads[0:latent, :] = grads[0:latent, :] + upper
            grads[latent : 2 * latent, :] = grads[latent : 2 * latent, :] + lower

        def node_terms():
            grad_kept[0] = pre_back
            grad_kept[1] = in_back
            if k == 0:
                grad_kept[2] = gained
                grad_mine = grad_own + grad_kept[2, own_rows, :]
            else:
                grad_mine = grad_own
            pre_mine = grad_kept[0, own_rows, :]
            row = lax.broadcasted_iota(jnp.int32, (8, LANES), 0)
            shifted = jnp.where(
                row == 2,
                jnp.sum(pre_mine, axis=0, keepdims=True),
                jnp.where(row == 3, jnp.sum(grad_mine, axis=0, keepdims=True), 0.0),
            )
            return (
                nn(nt(wide_pick, pre_mine.astype(BF16)).astype(BF16), node_kept[k, 0, own_rows, :]),
                nn(nt(wide_pick, grad_mine.astype(BF16)).astype(BF16), node_kept[k, 1, own_rows, :]),
                pltpu.roll(shifted, latent, 1),
                grad_mine + jnp.where(low_half, grad_kept[1, own_rows, :], 0.0),
            )

        if k == 0:
            first_terms, second_terms, node_bias, grad_own = node_terms()
            grads[2 * latent : 3 * latent, :] = grads[2 * latent : 3 * latent, :] + first_terms
            grads[3 * latent : 4 * latent, :] = grads[3 * latent : 4 * latent, :] + second_terms
            bias_at = slice(3 * latent, 3 * latent + 8)
            grads[bias_at, :] = grads[bias_at, :] + bias_terms + node_bias
            for at, (device, spot) in enumerate(plane_peers):
                send(
                    grads.at[pl.ds(pl.multiple_of(spot * shard, shard), shard), :],
                    plane_land.at[pl.ds(at * shard, shard), :],
                    6,
                    device,
                )

        back_send[k] = nt(
            onehot[2 * slab : 2 * slab + 2 * rim, :], back_stack[0 : 2 * latent, :]
        ).astype(BF16)
        send(back_send.at[k, 0:rim], back_land.at[k, 0:rim], 7 + k, (below, layer))
        send(
            back_send.at[k, rim : 2 * rim],
            back_land.at[k, rim : 2 * rim],
            7 + k,
            (above, layer),
        )
        from_source = nt(onehot[0:slab, :], back_stack[0 : 2 * latent, :])
        from_target = nt(onehot[slab : 2 * slab, :], back_stack[0 : 2 * latent, :])
        if k == 0:
            wait_bytes(plane_land, recv_sem.at[6])
            shard_rows = pl.ds(pl.multiple_of(plane_at * shard, shard), shard)
            total = grads[shard_rows, :]
            for turn in range(n_plane - 1):
                total = total + plane_land[turn * shard : (turn + 1) * shard, :]
            z_rows = pl.ds(pl.multiple_of(z_at * shard, shard), shard)
            z_land[z_rows, :] = total
            for peer in z_peers:
                send(z_land.at[z_rows, :], z_land.at[z_rows, :], 9, peer)
        wait_bytes(back_land.at[k], recv_sem.at[7 + k])
        from_source = (
            from_source
            + nn(rim_put[0], back_land[k, 0:rim])
            + nn(rim_put[1], back_land[k, rim : 2 * rim])
        )
        comb = jnp.where(low_half, from_source, from_target).astype(BF16)
        packed = nn(comb[0:half], first_back) + nn(comb[half:], first_back_high)
        if k == 1:
            swap(2, packed)
            upper, lower, bias_terms = weight_terms()
            first_terms, second_terms, node_bias, grad_own = node_terms()
            grads[0:latent, :] = upper
            grads[latent : 2 * latent, :] = lower
            grads[2 * latent : 3 * latent, :] = first_terms
            grads[3 * latent : 4 * latent, :] = second_terms
            bias_at = slice(3 * latent, 3 * latent + 8)
            grads[bias_at, :] = grads[bias_at, :] + bias_terms + node_bias
            node_kept[1, 0] = table
            node_out[...] = node_kept[1, 0, own_rows, 0:latent]

            def carried(cols):
                old = grad_edge[:, cols] + nn(self_back, back_stack[0:latent, cols])
                grad_edge[:, cols] = old
                second_grad_edge[:, cols] = nn(second_back, old.astype(BF16))

            chunks(slots, carried)
            cot_slab = pltpu.roll(slab_land[...].astype(F32), latent, 1)
            grad_before = jnp.where(low_half, cot_slab + in_back, 0.0)
            packed = swapped_sum(2)
            gained = jnp.concatenate(
                [
                    jnp.where(low_half, packed, 0.0),
                    jnp.where(low_half, pltpu.roll(packed, latent, 1), 0.0),
                ],
                axis=0,
            )
            grad_now = grad_before + gained
        else:
            comb_send[...] = packed.astype(BF16)

            def rows_of(device):
                return pl.ds(pl.multiple_of(lax.rem(device, n_layer // 2) * hits, hits), hits)

            for at, peer in enumerate(layer_peers):
                send(
                    comb_send.at[rows_of(peer), :],
                    comb_land.at[pl.ds(at * hits, hits), :],
                    10,
                    (phi, peer),
                )
            wait_bytes(z_land.at[pl.ds(0, (n_z - 1) * shard), :], recv_sem.at[9])
            total = z_land[0:shard, :]
            for turn in range(1, n_z):
                total = total + z_land[turn * shard : (turn + 1) * shard, :]
            grads_sum[shard_rows, :] = total
            for device, _ in plane_peers:
                send(grads_sum.at[shard_rows, :], grads_sum.at[shard_rows, :], 11, device)
            wait_bytes(comb_land, recv_sem.at[10])
            total = comb_send[rows_of(layer), :].astype(F32)
            for turn in range(n_layer - 1):
                total = total + comb_land[turn * hits : (turn + 1) * hits, :].astype(F32)
            total = jnp.where(layer < n_layer // 2, total, pltpu.roll(total, latent, 1))
            node_grad[...] = (grad_own + total)[:, 0:latent]

    wait_bytes(grads_sum.at[pl.ds(0, (n_plane - 1) * shard), :], recv_sem.at[11])
    grad_first[:, 0:LANES] = grads_sum[0:latent, :]
    grad_first[:, LANES:] = grads_sum[latent : 2 * latent, 0:latent]
    grad_second[...] = pltpu.roll(grads_sum[latent : 2 * latent, :], latent, 1)[:, 0:latent]
    grad_node_first[...] = grads_sum[2 * latent : 3 * latent, :]
    grad_node_second[...] = grads_sum[3 * latent : 4 * latent, 0:latent]
    grad_biases[...] = pltpu.roll(grads_sum[3 * latent : 3 * latent + 8, :], latent, 1)[
        0:4, 0:latent
    ]

    wait_bytes(slab_land.at[pl.ds(0, slab - hits), :], send_sem.at[0])
    for k in range(2):
        wait_bytes(rim_send.at[k], send_sem.at[1 + k])
        wait_bytes(back_send.at[k], send_sem.at[7 + k])
    for at in range(3):
        wait_bytes(swaps[at].at[pl.ds(0, (n_layer - 1) * half), :], send_sem.at[3 + at])
    wait_bytes(plane_land, send_sem.at[6])
    wait_bytes(z_land.at[pl.ds(0, (n_z - 1) * shard), :], send_sem.at[9])
    wait_bytes(comb_land, send_sem.at[10])
    wait_bytes(grads_sum.at[pl.ds(0, (n_plane - 1) * shard), :], send_sem.at[11])


def deliver(*refs):
    many = len(refs) // 2
    sems = refs[-1]
    copies = [
        pltpu.make_async_copy(refs[at], refs[many + at], sems.at[at]) for at in range(many)
    ]
    for copy in copies:
        copy.start()
    for copy in copies:
        copy.wait()


def body(n_phi, n_layer, *arrays):
    node_feats, edge_feats, edge_source, edge_target, *others, node_cot = arrays
    latent, hits = node_feats.shape
    slots = edge_feats.shape[1]
    slab = hits * n_layer
    rim = others[1].shape[1]
    n_plane = Y_LO * CORES * n_layer
    n_z = n_phi // (Y_LO * CORES)
    grad_rows = 4 * latent
    shard = grad_rows // n_plane
    vmem = pl.BlockSpec(memory_space=pltpu.VMEM)
    hbm = pl.BlockSpec(memory_space=pltpu.HBM)
    operands = (
        node_feats.T,
        edge_feats,
        edge_source.reshape(1, slots),
        edge_target.reshape(1, slots),
        *others,
        node_cot.T,
    )
    outs = [
        jax.ShapeDtypeStruct(*out)
        for out in (
            ((hits, latent), BF16),
            ((latent, slots), BF16),
            ((hits, latent), F32),
            ((latent, 3 * latent), F32),
            ((latent, latent), F32),
            ((latent, 2 * latent), F32),
            ((latent, latent), F32),
            ((4, latent), F32),
        )
    ]
    results = pl.pallas_call(
        functools.partial(kernel, n_phi, n_layer),
        out_shape=outs,
        in_specs=[hbm] * len(operands),
        out_specs=[vmem] * len(outs),
        scratch_shapes=[pltpu.VMEM(array.shape, array.dtype) for array in operands]
        + [
            pltpu.VMEM((2 * slab + 2 * rim, slots), BF16),
            pltpu.VMEM((2 * rim, slab), BF16),
            pltpu.VMEM((2, slab, rim), BF16),
            pltpu.VMEM((2, 4 * latent, slots), BF16),
            pltpu.VMEM((2, 2 * latent, slots), BF16),
            pltpu.VMEM((latent, slots), F32),
            pltpu.VMEM((2, latent, slots), F32),
            pltpu.VMEM((latent, slots), F32),
            pltpu.VMEM((latent, slots), F32),
            pltpu.VMEM((3 * latent, slots), BF16),
            pltpu.VMEM((2, 2, slab, LANES), BF16),
            pltpu.VMEM((3, slab, LANES), F32),
            pltpu.VMEM((hits, LANES), BF16),
            pltpu.VMEM((slab, LANES), BF16),
            pltpu.VMEM((2, 2 * rim, LANES), BF16),
            pltpu.VMEM((2, 2 * rim, LANES), BF16),
            pltpu.VMEM((n_layer * slab // 2, LANES), F32),
            pltpu.VMEM((2, n_layer * slab // 2, LANES), BF16),
            pltpu.VMEM((2, 2 * rim, LANES), BF16),
            pltpu.VMEM((2, 2 * rim, LANES), BF16),
            pltpu.VMEM((slab // 2, LANES), BF16),
            pltpu.VMEM(((n_layer - 1) * hits, LANES), BF16),
            pltpu.VMEM((grad_rows, LANES), F32),
            pltpu.VMEM(((n_plane - 1) * shard, LANES), F32),
            pltpu.VMEM((n_z * shard, LANES), F32),
            pltpu.VMEM((grad_rows, LANES), F32),
            pltpu.SemaphoreType.DMA((len(operands),)),
            pltpu.SemaphoreType.DMA((12,)),
            pltpu.SemaphoreType.DMA((12,)),
        ],
        compiler_params=pltpu.CompilerParams(
            collective_id=0, has_side_effects=True, vmem_limit_bytes=40 * 1024 * 1024
        ),
    )(*operands)
    node_out, edge_out, node_grad, *totals = pl.pallas_call(
        deliver,
        out_shape=outs,
        in_specs=[vmem] * len(outs),
        out_specs=[hbm] * len(outs),
        scratch_shapes=[pltpu.SemaphoreType.DMA((len(outs),))],
    )(*results)
    return node_out.T, edge_out, node_grad.T, *totals


def solution(mesh):
    split = P(None, ("phi", "layer"))
    return jax.shard_map(
        functools.partial(body, mesh.shape["phi"], mesh.shape["layer"]),
        mesh=mesh,
        in_specs=(
            split,
            split,
            P(("phi", "layer")),
            P(("phi", "layer")),
            P("phi", "layer"),
            P("phi", None),
            P("phi", None),
            P(),
            P(),
            P(),
            P(),
            P(),
            split,
        ),
        out_specs=(split, split, split, P(), P(), P(), P(), P()),
        check_vma=False,
    )
```

time: 1060 us -> 89.1 us (0.08)
  waiting for transfers between devices: 779 us -> 0 us
  blocking collectives: 113 us -> 0 us
  Pallas kernels: 0 us -> 74.9 us
  starting transfers between devices: 57.4 us -> 0 us
  local copies, waits for them, and re-layouts: 56.5 us -> 12.2 us
  matrix products: 18.7 us -> 0 us
  other arithmetic: 16 us -> 0 us
  between operations: 15.2 us -> 1.36 us
    psum x1 -> x0, waiting for transfers between devices: 447 us -> none  [body(): lax.psum((sum_first_edge, sum_second_edge, sum_first_node, sum_second_nod...]
    reduce_scatter x3 -> x0, waiting for transfers between devices: 247 us -> none  [the longest x2 163 us: body(): lax.psum_scatter(slab_grad.astype(jnp.bfloat16), 'layer', scatter_dimensi...]
    all_gather x4 -> x0, blocking collectives: 113 us -> none  [the longest x2 57.4 us: body(): slab_nodes = lax.all_gather(node_state, 'layer', axis=1, tiled=True)]
    unnamed x6 -> x0, waiting for transfers between devices: 84.5 us -> none
    pallas_call x0 -> x2, Pallas kernels: none -> 74.9 us  [the longest x1 73.1 us: body(): pl.pallas_call(functools.partial(kernel, n_phi, n_layer), out_shape=outs,...]
    ppermute x8 -> x0, starting transfers between devices: 57.2 us -> none  [from_behind(): return lax.ppermute(value, axis, pairs)]
    gather x14 -> x0, local copies, waits for them, and re-layouts: 40.6 us -> none  [the longest x4 12.8 us: body(): jnp.take(message_slab, edge_target, axis=1).astype(jnp.float32)]
    dot_general x51 -> x0, matrix products: 18.7 us -> none  [the longest x32 11.2 us: outer_dot(): lax.dot_general(left, right, (((1,), (1,)), ((), ())), preferred_element_...]
  transfers between devices with their start and end apart: 13 -> 0, of which waited for: 6 -> 0; matrix products, arithmetic and copies ran while one was open for 2% -> 0% of each run, Pallas kernels for 0% -> 0%
where the time goes in v1:
time: 89.1 us; the launch traced here: 88.4 us
  Pallas kernels  74.9 us (84%)
  local copies, waits for them, and re-layouts  12.2 us (14%)
  between operations  1.36 us (2%)
    pallas_call x1, Pallas kernels, body(): pl.pallas_call(functools.partial(kernel, n_phi, n_layer), out_shape=outs,...  73.1 us
    unnamed x40, local copies, waits for them, and re-layouts  12.2 us

profile of v1, /device:TPU:1, one launch (start us, length us, event | category | flops | bytes accessed | tf_op | source)
XLA Modules:
  0.0 88.4 jit_solution(10384078505906927659)
XLA Ops:
  0.6 0.0 copy-start.13
  1.3 0.0 copy-start.18
  1.3 0.0 copy-start.19
  1.3 0.0 copy-done.13
  1.3 0.6 copy-done.18
  2.0 0.0 copy-done.19
  2.0 0.0 copy-start.1
  2.0 0.9 %copy-done.1 = bf16[64,2048]{1,0:T(8,128)(2,1)S(1)} copy-done((bf16[64,2048]{1,0:T(8,128)(2,1)S(1)}, bf16[64,2048]{1,0:T(8,128)(2,1)}, u32[]{:S(2)}) %copy-start.1) | copy-done | bytes 262168
  2.9 0.0 copy-start.3
  2.9 0.8 copy-done.3
  3.7 0.0 copy-start.8
  3.7 0.7 copy-done.8
  4.4 0.0 copy-start.9
  4.4 0.7 copy-done.9
  5.1 0.0 copy-start.10
  5.1 0.7 copy-done.10
  5.8 0.0 copy-start.11
  5.8 0.7 copy-done.11
  6.6 0.0 copy-start.14
  6.6 0.7 copy-done.14
  7.3 0.0 copy-start.15
  7.3 0.7 copy-done.15
  8.0 0.0 copy-start.16
  8.0 0.7 copy-done.16
  8.6 73.1 %shard_map.188 = (bf16[32,64]{1,0:T(8,128)(2,1)S(1)}, bf16[64,2048]{1,0:T(8,128)(2,1)S(1)}, f32[32,64]{1,0:T(8,128)S(1)}, f32[64,192]{1,0:T(8,128)S(1)}, f32[64,...) custom-call(bf16[32,64]{1,0:T(8,128)(2,1)S(1)} %bitcast.7, ...), custom_call_target="tpu_custom_call" | custom-call | tf_op jit(solution)/shard_map/pallas_call | solution.py:648
  81.7 0.0 copy-start
  81.8 0.7 copy-done
  82.4 0.0 copy-start.2
  82.4 0.6 copy-done.2
  83.1 0.0 copy-start.4
  83.1 0.6 copy-done.4
  83.7 0.0 copy-start.5
  83.7 0.6 copy-done.5
  84.3 0.0 copy-start.6
  84.3 0.6 copy-done.6
  84.9 0.0 copy-start.7
  84.9 0.6 copy-done.7
  85.5 0.0 copy-start.12
  85.5 0.6 copy-done.12
  86.1 0.0 copy-start.17
  86.1 0.6 copy-done.17
  86.6 1.8 %shard_map.189 = (bf16[32,64]{1,0:T(8,128)(2,1)}, bf16[64,2048]{1,0:T(8,128)(2,1)}, f32[32,64]{1,0:T(8,128)}, f32[64,192]{1,0:T(8,128)}, f32[64,64]{1,0:T(8,128)...) custom-call(bf16[32,64]{1,0:T(8,128)(2,1)} %copy-done.12, bf16[64,2048]{1,0:T(8,128)(2,1)} %copy-done, ...), custom_call_target="tpu_custom_call" | custom-call | tf_op jit(solution)/shard_map/pallas_call | solution.py:689
Async XLA Ops:
  0.6 0.7 copy-start.13
  1.3 0.7 copy-start.18
  1.3 0.7 copy-start.19
  2.0 0.9 %copy-start.1 = (bf16[64,2048]{1,0:T(8,128)(2,1)S(1)}, bf16[64,2048]{1,0:T(8,128)(2,1)}, u32[]{:S(2)}) copy-start(bf16[64,2048]{1,0:T(8,128)(2,1)} %edges_in.1) | copy-start | bytes 786436
  2.9 0.8 copy-start.3
  3.7 0.7 copy-start.8
  4.4 0.7 copy-start.9
  5.1 0.7 copy-start.10
  5.8 0.7 copy-start.11
  6.6 0.7 copy-start.14
  7.3 0.7 copy-start.15
  8.0 0.7 copy-start.16
  81.7 0.7 copy-start
  82.4 0.6 copy-start.2
  83.1 0.6 copy-start.4
  83.7 0.6 copy-start.5
  84.3 0.6 copy-start.6
  84.9 0.6 copy-start.7
  85.5 0.6 copy-start.12
  86.1 0.6 copy-start.17

commit v2 on v1

--- a/solution.py
+++ b/solution.py
@@ -15,6 +15,7 @@
 Y_LO = 2
 CORES = 2
 CHUNK = 512
+VMEM_BYTES = 64 * 1024 * 1024
 
 
 def nn(left, right):
@@ -86,14 +87,14 @@
     node_second_in,
     biases_in,
     cot_in,
-    node_out,
-    edge_out,
-    node_grad,
-    grad_first,
-    grad_second,
-    grad_node_first,
-    grad_node_second,
-    grad_biases,
+    node_out_to,
+    edge_out_to,
+    node_grad_to,
+    grad_first_to,
+    grad_second_to,
+    grad_node_first_to,
+    grad_node_second_to,
+    grad_biases_to,
     feats,
     edges0,
     source,
@@ -107,6 +108,14 @@
     node_second,
     biases,
     cot,
+    node_out,
+    edge_out,
+    node_grad,
+    grad_first,
+    grad_second,
+    grad_node_first,
+    grad_node_second,
+    grad_biases,
     onehot,
     rim_pick,
     rim_put,
@@ -134,6 +143,8 @@
     z_land,
     grads_sum,
     load_sem,
+    store_sem,
+    chain_sem,
     send_sem,
     recv_sem,
 ):
@@ -191,9 +202,24 @@
         ).start()
 
     barrier = pltpu.get_barrier_semaphore()
-    greeted = z_peers + [device for device, _ in plane_peers] + [(above, layer), (below, layer)]
-    for device in greeted:
-        pl.semaphore_signal(barrier, inc=1, device_id=device, device_id_type=MESH)
+
+    def along_z(step):
+        return y_lo * (CORES * n_z) + lax.rem(z_at + step + n_z, n_z) * CORES + core, layer
+
+    def greet(sem, devices):
+        for device in devices:
+            pl.semaphore_signal(sem, inc=1, device_id=device, device_id_type=MESH)
+
+    greeted = [(phi, peer) for peer in layer_peers] + [
+        (phi_base[0] + 1 - core, layer),
+        (phi_base[0] + (1 - 2 * y_lo) * (CORES * n_z) + core, layer),
+        (phi_base[0] + (1 - 2 * y_lo) * (CORES * n_z) + 1 - core, layer),
+        (above, layer),
+        (below, layer),
+        along_z(1),
+        along_z(-1),
+    ]
+    greet(barrier, greeted)
 
     loads = [
         pltpu.make_async_copy(src, dst, load_sem.at[at])
@@ -231,10 +257,36 @@
         nn(feats[...], wide_pick) + nn(cot[...].astype(BF16), high_pick)
     ).astype(BF16)
     pl.semaphore_wait(barrier, len(greeted))
+    known = [step for step in (1, 2, 4) if step < n_z // 2]
+
+    def tell(at):
+        if at < len(known):
+            greet(chain_sem.at[at], [along_z(known[at]), along_z(-known[at])])
+
+    def told(at):
+        if at < len(known):
+            pl.semaphore_wait(chain_sem.at[at], 2)
+
+    tell(0)
     for peer in layer_peers:
         send(own_send, slab_land.at[own_rows, :], 0, (phi, peer))
     slab_land[own_rows, :] = own_send[...]
 
+    stores = [
+        pltpu.make_async_copy(src, dst, store_sem.at[at])
+        for at, (src, dst) in enumerate(
+            (
+                (node_out, node_out_to),
+                (edge_out, edge_out_to),
+                (node_grad, node_grad_to),
+                (grad_first, grad_first_to),
+                (grad_second, grad_second_to),
+                (grad_node_first, grad_node_first_to),
+                (grad_node_second, grad_node_second_to),
+                (grad_biases, grad_biases_to),
+            )
+        )
+    ]
     swaps = (message_land, swap_land.at[0], swap_land.at[1])
 
     def swap(at, value):
@@ -326,6 +378,8 @@
     )
 
     wait_bytes(slab_land.at[pl.ds(0, slab - hits), :], recv_sem.at[0])
+    told(0)
+    tell(1)
     table = jnp.where(low_half, slab_land[...].astype(F32), 0.0).astype(BF16)
     for k in range(2):
         rim_send[k] = nn(rim_pick[...], table).astype(BF16)
@@ -389,6 +443,9 @@
 
         chunks(slots, inputs)
         packed = swapped_sum(k)
+        told(1 + k)
+        if k == 0:
+            tell(2)
         turned = pltpu.roll(packed, latent, 1)
         table_wide = table.astype(F32)
         node_in = jnp.concatenate(
@@ -406,6 +463,8 @@
         node_kept[k, 1] = node_hidden
         if k == 0:
             first_slope = node_slope
+        else:
+            stores[1].start()
         table = (table_wide + nt(node_hidden, node_second_wide) + bias_update).astype(BF16)
 
     for k in (1, 0):
@@ -533,6 +592,7 @@
             grads[bias_at, :] = grads[bias_at, :] + bias_terms + node_bias
             node_kept[1, 0] = table
             node_out[...] = node_kept[1, 0, own_rows, 0:latent]
+            stores[0].start()
 
             def carried(cols):
                 old = grad_edge[:, cols] + nn(self_back, back_stack[0:latent, cols])
@@ -577,6 +637,7 @@
                 total = total + comb_land[turn * hits : (turn + 1) * hits, :].astype(F32)
             total = jnp.where(layer < n_layer // 2, total, pltpu.roll(total, latent, 1))
             node_grad[...] = (grad_own + total)[:, 0:latent]
+            stores[2].start()
 
     wait_bytes(grads_sum.at[pl.ds(0, (n_plane - 1) * shard), :], recv_sem.at[11])
     grad_first[:, 0:LANES] = grads_sum[0:latent, :]
@@ -587,6 +648,8 @@
     grad_biases[...] = pltpu.roll(grads_sum[3 * latent : 3 * latent + 8, :], latent, 1)[
         0:4, 0:latent
     ]
+    for store in stores[3:]:
+        store.start()
 
     wait_bytes(slab_land.at[pl.ds(0, slab - hits), :], send_sem.at[0])
     for k in range(2):
@@ -598,18 +661,26 @@
     wait_bytes(z_land.at[pl.ds(0, (n_z - 1) * shard), :], send_sem.at[9])
     wait_bytes(comb_land, send_sem.at[10])
     wait_bytes(grads_sum.at[pl.ds(0, (n_plane - 1) * shard), :], send_sem.at[11])
-
-
-def deliver(*refs):
-    many = len(refs) // 2
-    sems = refs[-1]
-    copies = [
-        pltpu.make_async_copy(refs[at], refs[many + at], sems.at[at]) for at in range(many)
-    ]
-    for copy in copies:
-        copy.start()
-    for copy in copies:
-        copy.wait()
+    for store in stores:
+        store.wait()
+
+
+def deliver(many, *refs):
+    sources, targets, held = refs[:many], refs[many : 2 * many], refs[2 * many : 3 * many]
+    in_sem, out_sem = refs[3 * many :]
+    loads = [
+        pltpu.make_async_copy(sources[at], held[at], in_sem.at[at]) for at in range(many)
+    ]
+    stores = [
+        pltpu.make_async_copy(held[at], targets[at], out_sem.at[at]) for at in range(many)
+    ]
+    for load in loads:
+        load.start()
+    for load, store in zip(loads, stores):
+        load.wait()
+        store.start()
+    for store in stores:
+        store.wait()
 
 
 def body(n_phi, n_layer, *arrays):
@@ -622,7 +693,6 @@
     n_z = n_phi // (Y_LO * CORES)
     grad_rows = 4 * latent
     shard = grad_rows // n_plane
-    vmem = pl.BlockSpec(memory_space=pltpu.VMEM)
     hbm = pl.BlockSpec(memory_space=pltpu.HBM)
     operands = (
         node_feats.T,
@@ -649,8 +719,8 @@
         functools.partial(kernel, n_phi, n_layer),
         out_shape=outs,
         in_specs=[hbm] * len(operands),
-        out_specs=[vmem] * len(outs),
-        scratch_shapes=[pltpu.VMEM(array.shape, array.dtype) for array in operands]
+        out_specs=[hbm] * len(outs),
+        scratch_shapes=[pltpu.VMEM(array.shape, array.dtype) for array in (*operands, *outs)]
         + [
             pltpu.VMEM((2 * slab + 2 * rim, slots), BF16),
             pltpu.VMEM((2 * rim, slab), BF16),
@@ -679,19 +749,23 @@
             pltpu.VMEM((n_z * shard, LANES), F32),
             pltpu.VMEM((grad_rows, LANES), F32),
             pltpu.SemaphoreType.DMA((len(operands),)),
+            pltpu.SemaphoreType.DMA((len(outs),)),
+            pltpu.SemaphoreType.REGULAR((3,)),
             pltpu.SemaphoreType.DMA((12,)),
             pltpu.SemaphoreType.DMA((12,)),
         ],
         compiler_params=pltpu.CompilerParams(
-            collective_id=0, has_side_effects=True, vmem_limit_bytes=40 * 1024 * 1024
+            collective_id=0, has_side_effects=True, vmem_limit_bytes=VMEM_BYTES
         ),
     )(*operands)
     node_out, edge_out, node_grad, *totals = pl.pallas_call(
-        deliver,
+        functools.partial(deliver, len(outs)),
         out_shape=outs,
-        in_specs=[vmem] * len(outs),
+        in_specs=[hbm] * len(outs),
         out_specs=[hbm] * len(outs),
-        scratch_shapes=[pltpu.SemaphoreType.DMA((len(outs),))],
+        scratch_shapes=[pltpu.VMEM(out.shape, out.dtype) for out in outs]
+        + [pltpu.SemaphoreType.DMA((len(outs),))] * 2,
+        compiler_params=pltpu.CompilerParams(vmem_limit_bytes=VMEM_BYTES),
     )(*results)
     return node_out.T, edge_out, node_grad.T, *totals
 

time: 89.1 us -> 75.1 us (0.84)
  local copies, waits for them, and re-layouts: 12.2 us -> 0 us
  Pallas kernels: 74.9 us -> 73.6 us
    unnamed x40 -> x0, local copies, waits for them, and re-layouts: 12.2 us -> none
    pallas_call x1, Pallas kernels: 73.1 us -> 71.7 us  [body(): pl.pallas_call(functools.partial(kernel, n_phi, n_layer), out_shape=outs,...]
where the time goes in v2:
time: 75.1 us; the launch traced here: 74.9 us
  Pallas kernels  73.6 us (98%)
  between operations  1.29 us (2%)
    pallas_call x1, Pallas kernels, body(): pl.pallas_call(functools.partial(kernel, n_phi, n_layer), out_shape=outs,...  71.7 us
    pallas_call x1, Pallas kernels, body(): pl.pallas_call(functools.partial(deliver, len(outs)), out_shape=outs, in_...  1.86 us

profile of v2, /device:TPU:1, one launch (start us, length us, event | category | flops | bytes accessed | tf_op | source)
XLA Modules:
  0.0 74.9 jit_solution(10870246461890453094)
XLA Ops:
  1.3 71.7 %shard_map.188 = (bf16[32,64]{1,0:T(8,128)(2,1)}, bf16[64,2048]{1,0:T(8,128)(2,1)}, f32[32,64]{1,0:T(8,128)}, f32[64,192]{1,0:T(8,128)}, f32[64,64]{1,0:T(8,128)...) custom-call(bf16[32,64]{1,0:T(8,128)(2,1)} %bitcast.7, bf16[64,2048]{1,0:T(8,128)(2,1)} %edges_in.1, ...), custom_call_target="tpu_custom_call" | custom-call | tf_op jit(solution)/shard_map/pallas_call | solution.py:718
  73.0 1.9 %shard_map.189 = (bf16[32,64]{1,0:T(8,128)(2,1)}, bf16[64,2048]{1,0:T(8,128)(2,1)}, f32[32,64]{1,0:T(8,128)}, f32[64,192]{1,0:T(8,128)}, f32[64,64]{1,0:T(8,128)...) custom-call(bf16[32,64]{1,0:T(8,128)(2,1)} %get-tuple-element.24.refs_0_, ...), custom_call_target="tpu_custom_call" | custom-call | tf_op jit(solution)/shard_map/pallas_call | solution.py:761

commit v3 on v2

--- a/solution.py
+++ b/solution.py
@@ -126,12 +126,19 @@
     grad_edge,
     second_grad_edge,
     back_stack,
+    bias_sums,
     node_kept,
     grad_kept,
     own_send,
     slab_land,
+    table_kept,
+    rim_near,
+    near_pick,
+    near_land,
+    pairs_land,
     rim_send,
     rim_land,
+    message_send,
     message_land,
     swap_land,
     back_send,
@@ -219,8 +226,6 @@
         along_z(1),
         along_z(-1),
     ]
-    greet(barrier, greeted)
-
     loads = [
         pltpu.make_async_copy(src, dst, load_sem.at[at])
         for at, (src, dst) in enumerate(
@@ -241,7 +246,10 @@
             )
         )
     ]
-    for load in loads:
+    for load in loads[:2]:
+        load.start()
+    greet(barrier, greeted)
+    for load in loads[2:]:
         load.start()
 
     lane = lax.broadcasted_iota(jnp.int32, (1, LANES), 1)
@@ -271,6 +279,8 @@
     for peer in layer_peers:
         send(own_send, slab_land.at[own_rows, :], 0, (phi, peer))
     slab_land[own_rows, :] = own_send[...]
+    send(rim_up_in, rim_near.at[0], 2, (above, layer))
+    send(rim_down_in, rim_near.at[1], 2, (below, layer))
 
     stores = [
         pltpu.make_async_copy(src, dst, store_sem.at[at])
@@ -287,7 +297,18 @@
             )
         )
     ]
-    swaps = (message_land, swap_land.at[0], swap_land.at[1])
+    swaps = (None, swap_land.at[0], swap_land.at[1])
+    x_rows = pl.ds(pl.multiple_of(x_at * hits, hits), hits)
+    lower_x_rows = pl.ds(pl.multiple_of(half + x_at * hits, hits), hits)
+    pair_rows = pl.ds(pl.multiple_of(x_at * 2 * hits, 2 * hits), 2 * hits)
+
+    def in_order(pairs):
+        parts = [
+            pairs[(2 * x + side) * hits : (2 * x + side + 1) * hits]
+            for side in range(2)
+            for x in range(n_x)
+        ]
+        return jnp.concatenate(parts, axis=0)
 
     def swap(at, value):
         swaps[at][swap_rows, :] = value.astype(swaps[at].dtype)
@@ -327,6 +348,8 @@
     node_first_wide = jnp.concatenate(
         [node_first[...], jnp.zeros((LANES - latent, 2 * latent), BF16)], axis=0
     )
+    gm_back = nt(gm_pick, node_first_wide)
+    gm_back = jnp.concatenate([gm_back[0:latent].astype(BF16), two_parts(gm_back[latent:])], axis=0)
     node_second_low = nn(node_second[...], wide_pick).astype(BF16)
     zero_wide = jnp.zeros((LANES - latent, LANES), BF16)
     node_second_wide = jnp.concatenate([node_second_low, zero_wide], axis=0)
@@ -381,15 +404,11 @@
     told(0)
     tell(1)
     table = jnp.where(low_half, slab_land[...].astype(F32), 0.0).astype(BF16)
+    rim_send[...] = nn(rim_pick[...], table).astype(BF16)
+    send(rim_send.at[0:rim], rim_land.at[0, 0:rim], 1, (above, layer))
+    send(rim_send.at[rim : 2 * rim], rim_land.at[0, rim : 2 * rim], 1, (below, layer))
+    table_kept[...] = table
     for k in range(2):
-        rim_send[k] = nn(rim_pick[...], table).astype(BF16)
-        send(rim_send.at[k, 0:rim], rim_land.at[k, 0:rim], 1 + k, (above, layer))
-        send(
-            rim_send.at[k, rim : 2 * rim],
-            rim_land.at[k, rim : 2 * rim],
-            1 + k,
-            (below, layer),
-        )
         own_part = two_parts(
             jnp.concatenate([nt(source_wide, table), nt(target_wide, table)], axis=1)
         )
@@ -399,7 +418,14 @@
             z_part[:, cols] = z_part[:, cols] + (terms[0:latent] + terms[latent:])
 
         chunks(slots, own_terms)
-        wait_bytes(rim_land.at[k], recv_sem.at[1 + k])
+        if k == 0:
+            wait_bytes(rim_land.at[0], recv_sem.at[1])
+        else:
+            wait_bytes(near_land, recv_sem.at[13])
+            for side in range(2):
+                rim_land[1, side * rim : (side + 1) * rim, :] = nn(
+                    near_pick[side * rim : (side + 1) * rim, :], near_land[side]
+                ).astype(BF16)
         rim_part = two_parts(nt(source_wide, rim_land[k]))
 
         def edge_mlp(cols):
@@ -420,7 +446,26 @@
 
         chunks(slots, edge_mlp)
         both_halves = nt(onehot[slab : 2 * slab, :], edge_new[k])
-        swap(k, jnp.where(low_half, both_halves[0:half], both_halves[half:]))
+        packed = jnp.where(low_half, both_halves[0:half], both_halves[half:])
+        if k == 0:
+            message_send[...] = packed
+            for peer in layer_peers:
+                spot = pl.ds(pl.multiple_of(lax.rem(peer, n_x) * hits, hits), hits)
+                send(message_send.at[spot, :], message_land.at[own_rows, :], 3, (phi, peer))
+            message_land[own_rows, :] = message_send[x_rows, :]
+            wait_bytes(rim_near, recv_sem.at[2])
+            row = lax.broadcasted_iota(jnp.int32, (slab, rim), 0)
+            pair_row = lax.rem(row, 2 * hits)
+            hit = (
+                lax.div(row, 2 * hits) * hits
+                + lax.rem(pair_row, hits)
+                + lax.div(pair_row, hits) * half
+            )
+            for side in range(2):
+                put = jnp.where(hit == rim_near[side], 1.0, 0.0).astype(BF16)
+                near_pick[side * rim : (side + 1) * rim, :] = nt(rim_eye, put).astype(BF16)
+        else:
+            swap(k, packed)
 
         raw_own = nt(wide_pick, table).astype(BF16)
         raw_rim = nt(wide_pick, rim_land[k]).astype(BF16)
@@ -442,16 +487,25 @@
             hidden_in[k, 2 * latent : 3 * latent, cols] = old
 
         chunks(slots, inputs)
-        packed = swapped_sum(k)
+        if k == 0:
+            wait_bytes(message_land.at[pl.ds(0, (n_layer - 1) * hits), :], recv_sem.at[3])
+            packed = message_land[0:hits, :]
+            for turn in range(1, n_layer):
+                packed = packed + message_land[turn * hits : (turn + 1) * hits, :]
+            upper_old = table_kept[x_rows, :].astype(F32)
+            lower_old = table_kept[lower_x_rows, :].astype(F32)
+        else:
+            packed = swapped_sum(k)
+            table_wide = table.astype(F32)
+            upper_old, lower_old = table_wide[0:half], table_wide[half:]
         told(1 + k)
         if k == 0:
             tell(2)
-        turned = pltpu.roll(packed, latent, 1)
-        table_wide = table.astype(F32)
+        node_old = jnp.concatenate([upper_old, lower_old], axis=0)
         node_in = jnp.concatenate(
             [
-                jnp.where(low_half, table_wide[0:half], turned),
-                jnp.where(low_half, table_wide[half:], packed),
+                jnp.where(low_half, upper_old, pltpu.roll(packed, latent, 1)),
+                jnp.where(low_half, lower_old, packed),
             ],
             axis=0,
         ).astype(BF16)
@@ -459,13 +513,27 @@
         node_gate = logistic(node_pre)
         node_hidden = (node_pre * node_gate).astype(BF16)
         node_slope = node_gate * (1.0 + node_pre * (1.0 - node_gate))
-        node_kept[k, 0] = node_in
-        node_kept[k, 1] = node_hidden
+        table = (node_old + nt(node_hidden, node_second_wide) + bias_update).astype(BF16)
         if k == 0:
-            first_slope = node_slope
+            turned = pltpu.roll(node_slope, latent, 1)
+            pairs_land[pair_rows, :] = jnp.where(low_half, table.astype(F32), turned).astype(BF16)
+            mine = pairs_land.at[pair_rows, :]
+            for side, slab_at in enumerate((above, below)):
+                for x in x_of:
+                    send(mine, near_land.at[side, pair_rows, :], 13, (slab_at, y_hi * n_x + x))
+            for (step,) in far_first((n_x,)):
+                send(mine, mine, 12, (phi, y_hi * n_x + x_of[step]))
+            node_kept[0, 0, 0 : 2 * hits] = node_in
+            node_kept[0, 1, 0 : 2 * hits] = node_hidden
+            if n_x > 1:
+                wait_bytes(pairs_land.at[pl.ds(0, (n_x - 1) * 2 * hits), :], recv_sem.at[12])
+            gathered = in_order(pairs_land[...].astype(F32))
+            table = jnp.where(low_half, gathered, 0.0).astype(BF16)
+            first_slope = pltpu.roll(gathered, latent, 1)
         else:
+            node_kept[1, 0] = node_in
+            node_kept[1, 1] = node_hidden
             stores[1].start()
-        table = (table_wide + nt(node_hidden, node_second_wide) + bias_update).astype(BF16)
 
     for k in (1, 0):
         if k == 1:
@@ -475,8 +543,23 @@
             pre_back = nn(grad_low, node_second_wide) * first_slope
         pre_low = pre_back.astype(BF16)
         in_back = nn(pre_low, node_first_wide)
-        gm_part = nt(gm_pick, in_back.astype(BF16))
-        gm_part = jnp.concatenate([gm_part[0:latent].astype(BF16), two_parts(gm_part[latent:])], axis=0)
+        gm_part = nt(gm_back, pre_low)
+        gm_part = jnp.concatenate(
+            [
+                gm_part[0:latent].astype(BF16),
+                two_parts(gm_part[latent : 2 * latent] + gm_part[2 * latent :]),
+            ],
+            axis=0,
+        )
+
+        if k == 1:
+            bias_sums[...] = jnp.zeros_like(bias_sums)
+
+        def folded(value):
+            pieces = [
+                value[:, at : at + LANES] for at in range(0, value.shape[1], LANES)
+            ]
+            return functools.reduce(lambda one, other: one + other, pieces)
 
         def edge_back(cols):
             both = nn(gm_part, onehot[slab : 2 * slab, cols])
@@ -487,7 +570,10 @@
                 hidden_grad = hidden_grad + second_grad_edge[:, cols]
             else:
                 grad_edge[:, cols] = edge_grad
-            pre_grad = (hidden_grad * slopes[k, :, cols]).astype(BF16)
+            pre_grad = hidden_grad * slopes[k, :, cols]
+            bias_sums[0] = bias_sums[0] + folded(pre_grad)
+            bias_sums[1] = bias_sums[1] + folded(edge_grad)
+            pre_grad = pre_grad.astype(BF16)
             back_stack[0:latent, cols] = pre_grad
             back_stack[latent : 2 * latent, cols] = pre_grad
             back_stack[2 * latent : 3 * latent, cols] = edge_grad.astype(BF16)
@@ -498,23 +584,20 @@
             outer = nt(back_stack[latent : 3 * latent, :], hidden_in[k])
             upper = outer[0:latent, 0:LANES]
             lower = jnp.where(low_half, outer[0:latent, LANES:], outer[latent:, LANES:])
-            ones = jnp.ones((8, slots), BF16)
-            pre_sums = nt(ones, back_stack[0 : 2 * latent, :])
-            edge_sums = nt(ones, back_stack[latent : 3 * latent, :])
-            row = lax.broadcasted_iota(jnp.int32, (8, LANES), 0)
-            bias_terms = jnp.where(
-                low_half,
-                0.0,
-                jnp.where(row == 0, pre_sums, jnp.where(row == 1, edge_sums, 0.0)),
-            )
-            return upper, lower, bias_terms
+            return upper, lower
+
+        def column_at(at, sums):
+            return jnp.where(lane == latent + at, jnp.sum(sums, axis=1, keepdims=True), 0.0)
 
         if k == 0:
-            upper, lower, bias_terms = weight_terms()
+            upper, lower = weight_terms()
             grads[0:latent, :] = grads[0:latent, :] + upper
             grads[latent : 2 * latent, :] = grads[latent : 2 * latent, :] + lower
 
         def node_terms():
+            kept_rows = (
+                pl.ds(pl.multiple_of(y_hi * hits, hits), hits) if k == 0 else own_rows
+            )
             grad_kept[0] = pre_back
             grad_kept[1] = in_back
             if k == 0:
@@ -523,25 +606,25 @@
             else:
                 grad_mine = grad_own
             pre_mine = grad_kept[0, own_rows, :]
-            row = lax.broadcasted_iota(jnp.int32, (8, LANES), 0)
-            shifted = jnp.where(
-                row == 2,
-                jnp.sum(pre_mine, axis=0, keepdims=True),
-                jnp.where(row == 3, jnp.sum(grad_mine, axis=0, keepdims=True), 0.0),
-            )
+            pre_turned = nt(wide_pick, pre_mine.astype(BF16))
+            grad_turned = nt(wide_pick, grad_mine.astype(BF16))
             return (
-                nn(nt(wide_pick, pre_mine.astype(BF16)).astype(BF16), node_kept[k, 0, own_rows, :]),
-                nn(nt(wide_pick, grad_mine.astype(BF16)).astype(BF16), node_kept[k, 1, own_rows, :]),
-                pltpu.roll(shifted, latent, 1),
+                nn(pre_turned.astype(BF16), node_kept[k, 0, kept_rows, :]),
+                nn(grad_turned.astype(BF16), node_kept[k, 1, kept_rows, :])
+                + column_at(2, pre_turned)
+                + column_at(3, grad_turned),
                 grad_mine + jnp.where(low_half, grad_kept[1, own_rows, :], 0.0),
             )
 
         if k == 0:
-            first_terms, second_terms, node_bias, grad_own = node_terms()
+            first_terms, second_terms, grad_own = node_terms()
             grads[2 * latent : 3 * latent, :] = grads[2 * latent : 3 * latent, :] + first_terms
-            grads[3 * latent : 4 * latent, :] = grads[3 * latent : 4 * latent, :] + second_terms
-            bias_at = slice(3 * latent, 3 * latent + 8)
-            grads[bias_at, :] = grads[bias_at, :] + bias_terms + node_bias
+            grads[3 * latent : 4 * latent, :] = (
+                grads[3 * latent : 4 * latent, :]
+                + second_terms
+                + column_at(0, bias_sums[0])
+                + column_at(1, bias_sums[1])
+            )
             for at, (device, spot) in enumerate(plane_peers):
                 send(
                     grads.at[pl.ds(pl.multiple_of(spot * shard, shard), shard), :],
@@ -582,14 +665,12 @@
         packed = nn(comb[0:half], first_back) + nn(comb[half:], first_back_high)
         if k == 1:
             swap(2, packed)
-            upper, lower, bias_terms = weight_terms()
-            first_terms, second_terms, node_bias, grad_own = node_terms()
+            upper, lower = weight_terms()
+            first_terms, second_terms, grad_own = node_terms()
             grads[0:latent, :] = upper
             grads[latent : 2 * latent, :] = lower
             grads[2 * latent : 3 * latent, :] = first_terms
             grads[3 * latent : 4 * latent, :] = second_terms
-            bias_at = slice(3 * latent, 3 * latent + 8)
-            grads[bias_at, :] = grads[bias_at, :] + bias_terms + node_bias
             node_kept[1, 0] = table
             node_out[...] = node_kept[1, 0, own_rows, 0:latent]
             stores[0].start()
@@ -645,17 +726,20 @@
     grad_second[...] = pltpu.roll(grads_sum[latent : 2 * latent, :], latent, 1)[:, 0:latent]
     grad_node_first[...] = grads_sum[2 * latent : 3 * latent, :]
     grad_node_second[...] = grads_sum[3 * latent : 4 * latent, 0:latent]
-    grad_biases[...] = pltpu.roll(grads_sum[3 * latent : 3 * latent + 8, :], latent, 1)[
-        0:4, 0:latent
-    ]
+    grad_biases[...] = grads_sum[3 * latent : 4 * latent, :].T[latent : latent + 4, :]
     for store in stores[3:]:
         store.start()
 
     wait_bytes(slab_land.at[pl.ds(0, slab - hits), :], send_sem.at[0])
+    wait_bytes(rim_send, send_sem.at[1])
+    wait_bytes(rim_near, send_sem.at[2])
+    wait_bytes(message_land.at[pl.ds(0, (n_layer - 1) * hits), :], send_sem.at[3])
+    if n_x > 1:
+        wait_bytes(pairs_land.at[pl.ds(0, (n_x - 1) * 2 * hits), :], send_sem.at[12])
+    wait_bytes(near_land, send_sem.at[13])
     for k in range(2):
-        wait_bytes(rim_send.at[k], send_sem.at[1 + k])
         wait_bytes(back_send.at[k], send_sem.at[7 + k])
-    for at in range(3):
+    for at in range(1, 3):
         wait_bytes(swaps[at].at[pl.ds(0, (n_layer - 1) * half), :], send_sem.at[3 + at])
     wait_bytes(plane_land, send_sem.at[6])
     wait_bytes(z_land.at[pl.ds(0, (n_z - 1) * shard), :], send_sem.at[9])
@@ -732,13 +816,20 @@
             pltpu.VMEM((latent, slots), F32),
             pltpu.VMEM((latent, slots), F32),
             pltpu.VMEM((3 * latent, slots), BF16),
+            pltpu.VMEM((2, latent, LANES), F32),
             pltpu.VMEM((2, 2, slab, LANES), BF16),
             pltpu.VMEM((3, slab, LANES), F32),
             pltpu.VMEM((hits, LANES), BF16),
             pltpu.VMEM((slab, LANES), BF16),
+            pltpu.VMEM((slab, LANES), BF16),
+            pltpu.VMEM((2, 1, rim), jnp.int32),
+            pltpu.VMEM((2 * rim, slab), BF16),
+            pltpu.VMEM((2, slab, LANES), BF16),
+            pltpu.VMEM((slab, LANES), BF16),
+            pltpu.VMEM((2 * rim, LANES), BF16),
             pltpu.VMEM((2, 2 * rim, LANES), BF16),
-            pltpu.VMEM((2, 2 * rim, LANES), BF16),
-            pltpu.VMEM((n_layer * slab // 2, LANES), F32),
+            pltpu.VMEM((slab // 2, LANES), F32),
+            pltpu.VMEM((slab, LANES), F32),
             pltpu.VMEM((2, n_layer * slab // 2, LANES), BF16),
             pltpu.VMEM((2, 2 * rim, LANES), BF16),
             pltpu.VMEM((2, 2 * rim, LANES), BF16),
@@ -751,8 +842,8 @@
             pltpu.SemaphoreType.DMA((len(operands),)),
             pltpu.SemaphoreType.DMA((len(outs),)),
             pltpu.SemaphoreType.REGULAR((3,)),
-            pltpu.SemaphoreType.DMA((12,)),
-            pltpu.SemaphoreType.DMA((12,)),
+            pltpu.SemaphoreType.DMA((14,)),
+            pltpu.SemaphoreType.DMA((14,)),
         ],
         compiler_params=pltpu.CompilerParams(
             collective_id=0, has_side_effects=True, vmem_limit_bytes=VMEM_BYTES

time: 75.1 us -> 74 us (0.985)
  Pallas kernels: 73.6 us -> 72.5 us
    pallas_call x1, Pallas kernels: 71.7 us -> 70.6 us  [body(): pl.pallas_call(functools.partial(kernel, n_phi, n_layer), out_shape=outs,...]
where the time goes in v3:
time: 74 us; the launch traced here: 73.8 us
  Pallas kernels  72.5 us (98%)
  between operations  1.29 us (2%)
    pallas_call x1, Pallas kernels, body(): pl.pallas_call(functools.partial(kernel, n_phi, n_layer), out_shape=outs,...  70.6 us
    pallas_call x1, Pallas kernels, body(): pl.pallas_call(functools.partial(deliver, len(outs)), out_shape=outs, in_...  1.86 us

profile of v3, /device:TPU:1, one launch (start us, length us, event | category | flops | bytes accessed | tf_op | source)
XLA Modules:
  0.0 73.8 jit_solution(12738893055008639254)
XLA Ops:
  1.3 70.6 %shard_map.188 = (bf16[32,64]{1,0:T(8,128)(2,1)}, bf16[64,2048]{1,0:T(8,128)(2,1)}, f32[32,64]{1,0:T(8,128)}, f32[64,192]{1,0:T(8,128)}, f32[64,64]{1,0:T(8,128)...) custom-call(bf16[32,64]{1,0:T(8,128)(2,1)} %bitcast.7, bf16[64,2048]{1,0:T(8,128)(2,1)} %edges_in.1, ...), custom_call_target="tpu_custom_call" | custom-call | tf_op jit(solution)/shard_map/pallas_call | solution.py:802
  71.9 1.9 %shard_map.189 = (bf16[32,64]{1,0:T(8,128)(2,1)}, bf16[64,2048]{1,0:T(8,128)(2,1)}, f32[32,64]{1,0:T(8,128)}, f32[64,192]{1,0:T(8,128)}, f32[64,64]{1,0:T(8,128)...) custom-call(bf16[32,64]{1,0:T(8,128)(2,1)} %get-tuple-element.24.refs_0_, ...), custom_call_target="tpu_custom_call" | custom-call | tf_op jit(solution)/shard_map/pallas_call | solution.py:852

commit v4 on v3

--- a/solution.py
+++ b/solution.py
@@ -14,7 +14,7 @@
 LANES = 128
 Y_LO = 2
 CORES = 2
-CHUNK = 512
+CHUNK = 1024
 VMEM_BYTES = 64 * 1024 * 1024
 
 
@@ -90,11 +90,7 @@
     node_out_to,
     edge_out_to,
     node_grad_to,
-    grad_first_to,
-    grad_second_to,
-    grad_node_first_to,
-    grad_node_second_to,
-    grad_biases_to,
+    sums_to,
     feats,
     edges0,
     source,
@@ -111,11 +107,6 @@
     node_out,
     edge_out,
     node_grad,
-    grad_first,
-    grad_second,
-    grad_node_first,
-    grad_node_second,
-    grad_biases,
     onehot,
     rim_pick,
     rim_put,
@@ -148,7 +139,7 @@
     grads,
     plane_land,
     z_land,
-    grads_sum,
+    shard_sum,
     load_sem,
     store_sem,
     chain_sem,
@@ -282,6 +273,7 @@
     send(rim_up_in, rim_near.at[0], 2, (above, layer))
     send(rim_down_in, rim_near.at[1], 2, (below, layer))
 
+    shard_rows = pl.ds(pl.multiple_of(plane_at * shard, shard), shard)
     stores = [
         pltpu.make_async_copy(src, dst, store_sem.at[at])
         for at, (src, dst) in enumerate(
@@ -289,11 +281,7 @@
                 (node_out, node_out_to),
                 (edge_out, edge_out_to),
                 (node_grad, node_grad_to),
-                (grad_first, grad_first_to),
-                (grad_second, grad_second_to),
-                (grad_node_first, grad_node_first_to),
-                (grad_node_second, grad_node_second_to),
-                (grad_biases, grad_biases_to),
+                (shard_sum, sums_to.at[shard_rows, :]),
             )
         )
     ]
@@ -403,10 +391,10 @@
     wait_bytes(slab_land.at[pl.ds(0, slab - hits), :], recv_sem.at[0])
     told(0)
     tell(1)
-    table = jnp.where(low_half, slab_land[...].astype(F32), 0.0).astype(BF16)
-    rim_send[...] = nn(rim_pick[...], table).astype(BF16)
+    rim_send[...] = nn(rim_pick[...], slab_land[...]).astype(BF16)
     send(rim_send.at[0:rim], rim_land.at[0, 0:rim], 1, (above, layer))
     send(rim_send.at[rim : 2 * rim], rim_land.at[0, rim : 2 * rim], 1, (below, layer))
+    table = jnp.where(low_half, slab_land[...].astype(F32), 0.0).astype(BF16)
     table_kept[...] = table
     for k in range(2):
         own_part = two_parts(
@@ -442,11 +430,10 @@
                 here, old.astype(F32) + nn(edge_second, hidden) + bias_message, 0.0
             ).astype(BF16)
             edge_new[k, 0:latent, cols] = fresh
-            edge_new[k, latent : 2 * latent, cols] = fresh
 
         chunks(slots, edge_mlp)
         both_halves = nt(onehot[slab : 2 * slab, :], edge_new[k])
-        packed = jnp.where(low_half, both_halves[0:half], both_halves[half:])
+        packed = jnp.concatenate([both_halves[0:half], both_halves[half:]], axis=1)
         if k == 0:
             message_send[...] = packed
             for peer in layer_peers:
@@ -647,7 +634,6 @@
         from_target = nt(onehot[slab : 2 * slab, :], back_stack[0 : 2 * latent, :])
         if k == 0:
             wait_bytes(plane_land, recv_sem.at[6])
-            shard_rows = pl.ds(pl.multiple_of(plane_at * shard, shard), shard)
             total = grads[shard_rows, :]
             for turn in range(n_plane - 1):
                 total = total + plane_land[turn * shard : (turn + 1) * shard, :]
@@ -709,9 +695,10 @@
             total = z_land[0:shard, :]
             for turn in range(1, n_z):
                 total = total + z_land[turn * shard : (turn + 1) * shard, :]
-            grads_sum[shard_rows, :] = total
+            shard_sum[...] = total
             for device, _ in plane_peers:
-                send(grads_sum.at[shard_rows, :], grads_sum.at[shard_rows, :], 11, device)
+                send(shard_sum, sums_to.at[shard_rows, :], 11, device)
+            stores[3].start()
             wait_bytes(comb_land, recv_sem.at[10])
             total = comb_send[rows_of(layer), :].astype(F32)
             for turn in range(n_layer - 1):
@@ -720,16 +707,7 @@
             node_grad[...] = (grad_own + total)[:, 0:latent]
             stores[2].start()
 
-    wait_bytes(grads_sum.at[pl.ds(0, (n_plane - 1) * shard), :], recv_sem.at[11])
-    grad_first[:, 0:LANES] = grads_sum[0:latent, :]
-    grad_first[:, LANES:] = grads_sum[latent : 2 * latent, 0:latent]
-    grad_second[...] = pltpu.roll(grads_sum[latent : 2 * latent, :], latent, 1)[:, 0:latent]
-    grad_node_first[...] = grads_sum[2 * latent : 3 * latent, :]
-    grad_node_second[...] = grads_sum[3 * latent : 4 * latent, 0:latent]
-    grad_biases[...] = grads_sum[3 * latent : 4 * latent, :].T[latent : latent + 4, :]
-    for store in stores[3:]:
-        store.start()
-
+    wait_bytes(sums_to.at[pl.ds(0, (n_plane - 1) * shard), :], recv_sem.at[11])
     wait_bytes(slab_land.at[pl.ds(0, slab - hits), :], send_sem.at[0])
     wait_bytes(rim_send, send_sem.at[1])
     wait_bytes(rim_near, send_sem.at[2])
@@ -744,23 +722,35 @@
     wait_bytes(plane_land, send_sem.at[6])
     wait_bytes(z_land.at[pl.ds(0, (n_z - 1) * shard), :], send_sem.at[9])
     wait_bytes(comb_land, send_sem.at[10])
-    wait_bytes(grads_sum.at[pl.ds(0, (n_plane - 1) * shard), :], send_sem.at[11])
+    wait_bytes(plane_land, send_sem.at[11])
     for store in stores:
         store.wait()
 
 
-def deliver(many, *refs):
-    sources, targets, held = refs[:many], refs[many : 2 * many], refs[2 * many : 3 * many]
-    in_sem, out_sem = refs[3 * many :]
+def deliver(*refs):
+    sources, targets, held, sums = refs[:4], refs[4:12], refs[12:20], refs[20]
+    in_sem, out_sem = refs[21:]
+    first, second, node_first, node_second, biases = held[3:]
+    latent = second.shape[0]
     loads = [
-        pltpu.make_async_copy(sources[at], held[at], in_sem.at[at]) for at in range(many)
+        pltpu.make_async_copy(sources[at], dst, in_sem.at[at])
+        for at, dst in enumerate((*held[:3], sums))
     ]
     stores = [
-        pltpu.make_async_copy(held[at], targets[at], out_sem.at[at]) for at in range(many)
+        pltpu.make_async_copy(held[at], targets[at], out_sem.at[at]) for at in range(8)
     ]
     for load in loads:
         load.start()
-    for load, store in zip(loads, stores):
+    loads[3].wait()
+    first[:, 0:LANES] = sums[0:latent, :]
+    first[:, LANES:] = sums[latent : 2 * latent, 0:latent]
+    second[...] = pltpu.roll(sums[latent : 2 * latent, :], latent, 1)[:, 0:latent]
+    node_first[...] = sums[2 * latent : 3 * latent, :]
+    node_second[...] = sums[3 * latent : 4 * latent, 0:latent]
+    biases[...] = sums[3 * latent : 4 * latent, :].T[latent : latent + 4, :]
+    for store in stores[3:]:
+        store.start()
+    for load, store in zip(loads[:3], stores):
         load.wait()
         store.start()
     for store in stores:
@@ -801,16 +791,16 @@
     ]
     results = pl.pallas_call(
         functools.partial(kernel, n_phi, n_layer),
-        out_shape=outs,
+        out_shape=[*outs[:3], jax.ShapeDtypeStruct((grad_rows, LANES), F32)],
         in_specs=[hbm] * len(operands),
-        out_specs=[hbm] * len(outs),
-        scratch_shapes=[pltpu.VMEM(array.shape, array.dtype) for array in (*operands, *outs)]
+        out_specs=[hbm] * 4,
+        scratch_shapes=[pltpu.VMEM(array.shape, array.dtype) for array in (*operands, *outs[:3])]
         + [
             pltpu.VMEM((2 * slab + 2 * rim, slots), BF16),
             pltpu.VMEM((2 * rim, slab), BF16),
             pltpu.VMEM((2, slab, rim), BF16),
             pltpu.VMEM((2, 4 * latent, slots), BF16),
-            pltpu.VMEM((2, 2 * latent, slots), BF16),
+            pltpu.VMEM((2, latent, slots), BF16),
             pltpu.VMEM((latent, slots), F32),
             pltpu.VMEM((2, latent, slots), F32),
             pltpu.VMEM((latent, slots), F32),
@@ -838,9 +828,9 @@
             pltpu.VMEM((grad_rows, LANES), F32),
             pltpu.VMEM(((n_plane - 1) * shard, LANES), F32),
             pltpu.VMEM((n_z * shard, LANES), F32),
-            pltpu.VMEM((grad_rows, LANES), F32),
+            pltpu.VMEM((shard, LANES), F32),
             pltpu.SemaphoreType.DMA((len(operands),)),
-            pltpu.SemaphoreType.DMA((len(outs),)),
+            pltpu.SemaphoreType.DMA((4,)),
             pltpu.SemaphoreType.REGULAR((3,)),
             pltpu.SemaphoreType.DMA((14,)),
             pltpu.SemaphoreType.DMA((14,)),
@@ -850,12 +840,16 @@
         ),
     )(*operands)
     node_out, edge_out, node_grad, *totals = pl.pallas_call(
-        functools.partial(deliver, len(outs)),
+        deliver,
         out_shape=outs,
-        in_specs=[hbm] * len(outs),
+        in_specs=[hbm] * 4,
         out_specs=[hbm] * len(outs),
         scratch_shapes=[pltpu.VMEM(out.shape, out.dtype) for out in outs]
-        + [pltpu.SemaphoreType.DMA((len(outs),))] * 2,
+        + [
+            pltpu.VMEM((grad_rows, LANES), F32),
+            pltpu.SemaphoreType.DMA((4,)),
+            pltpu.SemaphoreType.DMA((len(outs),)),
+        ],
         compiler_params=pltpu.CompilerParams(vmem_limit_bytes=VMEM_BYTES),
     )(*results)
     return node_out.T, edge_out, node_grad.T, *totals

time: 74 us -> 73 us (0.986)
  Pallas kernels: 72.5 us -> 71.5 us
    pallas_call x2, Pallas kernels: 72.5 us -> 71.5 us  [the longest x1 69.6 us: body(): pl.pallas_call(functools.partial(kernel, n_phi, n_layer), out_shape=[*out...]
where the time goes in v4:
time: 73 us; the launch traced here: 72.8 us
  Pallas kernels  71.5 us (98%)
  between operations  1.29 us (2%)
    pallas_call x1, Pallas kernels, body(): pl.pallas_call(functools.partial(kernel, n_phi, n_layer), out_shape=[*out...  69.6 us
    pallas_call x1, Pallas kernels, body(): pl.pallas_call(deliver, out_shape=outs, in_specs=[hbm] * 4, out_specs=[hb...  1.95 us

profile of v4, /device:TPU:1, one launch (start us, length us, event | category | flops | bytes accessed | tf_op | source)
XLA Modules:
  0.0 72.8 jit_solution(11734092145742899054)
XLA Ops:
  1.3 69.6 %shard_map.188 = (bf16[32,64]{1,0:T(8,128)(2,1)}, bf16[64,2048]{1,0:T(8,128)(2,1)}, f32[32,64]{1,0:T(8,128)}, f32[256,128]{1,0:T(8,128)}) custom-call(bf16[32,64]{1,0:T(8,128)(2,1)} %bitcast.7, bf16[64,2048]{1,0:T(8,128)(2,1)} %edges_in.1, s32[1,2048]{1,0:T(1,128)} %bitcast.8, s32[1,2048]{1,0:T(1,128)} %bitcast.9, s32[1,1]{1,0:T(1,128)S(6)} %copy.21.count_in, ...), custom_call_target="tpu_custom_call" | custom-call | tf_op jit(solution)/shard_map/pallas_call | solution.py:792
  70.9 2.0 %shard_map.189 = (bf16[32,64]{1,0:T(8,128)(2,1)}, bf16[64,2048]{1,0:T(8,128)(2,1)}, f32[32,64]{1,0:T(8,128)}, f32[64,192]{1,0:T(8,128)}, f32[64,64]{1,0:T(8,128)...) custom-call(bf16[32,64]{1,0:T(8,128)(2,1)} %get-tuple-element.20.refs_0_, ...), custom_call_target="tpu_custom_call" | custom-call | tf_op jit(solution)/shard_map/pallas_call | solution.py:842

commit v5 on v4

--- a/solution.py
+++ b/solution.py
@@ -237,10 +237,8 @@
             )
         )
     ]
-    for load in loads[:2]:
-        load.start()
     greet(barrier, greeted)
-    for load in loads[2:]:
+    for load in loads:
         load.start()
 
     lane = lax.broadcasted_iota(jnp.int32, (1, LANES), 1)
@@ -505,11 +503,11 @@
             turned = pltpu.roll(node_slope, latent, 1)
             pairs_land[pair_rows, :] = jnp.where(low_half, table.astype(F32), turned).astype(BF16)
             mine = pairs_land.at[pair_rows, :]
-            for side, slab_at in enumerate((above, below)):
-                for x in x_of:
-                    send(mine, near_land.at[side, pair_rows, :], 13, (slab_at, y_hi * n_x + x))
             for (step,) in far_first((n_x,)):
                 send(mine, mine, 12, (phi, y_hi * n_x + x_of[step]))
+            for x in x_of[::-1]:
+                for side, slab_at in enumerate((above, below)):
+                    send(mine, near_land.at[side, pair_rows, :], 13, (slab_at, y_hi * n_x + x))
             node_kept[0, 0, 0 : 2 * hits] = node_in
             node_kept[0, 1, 0 : 2 * hits] = node_hidden
             if n_x > 1:
@@ -539,47 +537,8 @@
             axis=0,
         )
 
-        if k == 1:
-            bias_sums[...] = jnp.zeros_like(bias_sums)
-
-        def folded(value):
-            pieces = [
-                value[:, at : at + LANES] for at in range(0, value.shape[1], LANES)
-            ]
-            return functools.reduce(lambda one, other: one + other, pieces)
-
-        def edge_back(cols):
-            both = nn(gm_part, onehot[slab : 2 * slab, cols])
-            edge_grad = both[0:latent]
-            hidden_grad = both[latent : 2 * latent] + both[2 * latent :]
-            if k == 0:
-                edge_grad = edge_grad + grad_edge[:, cols]
-                hidden_grad = hidden_grad + second_grad_edge[:, cols]
-            else:
-                grad_edge[:, cols] = edge_grad
-            pre_grad = hidden_grad * slopes[k, :, cols]
-            bias_sums[0] = bias_sums[0] + folded(pre_grad)
-            bias_sums[1] = bias_sums[1] + folded(edge_grad)
-            pre_grad = pre_grad.astype(BF16)
-            back_stack[0:latent, cols] = pre_grad
-            back_stack[latent : 2 * latent, cols] = pre_grad
-            back_stack[2 * latent : 3 * latent, cols] = edge_grad.astype(BF16)
-
-        chunks(slots, edge_back)
-
-        def weight_terms():
-            outer = nt(back_stack[latent : 3 * latent, :], hidden_in[k])
-            upper = outer[0:latent, 0:LANES]
-            lower = jnp.where(low_half, outer[0:latent, LANES:], outer[latent:, LANES:])
-            return upper, lower
-
         def column_at(at, sums):
             return jnp.where(lane == latent + at, jnp.sum(sums, axis=1, keepdims=True), 0.0)
-
-        if k == 0:
-            upper, lower = weight_terms()
-            grads[0:latent, :] = grads[0:latent, :] + upper
-            grads[latent : 2 * latent, :] = grads[latent : 2 * latent, :] + lower
 
         def node_terms():
             kept_rows = (
@@ -603,12 +562,52 @@
                 grad_mine + jnp.where(low_half, grad_kept[1, own_rows, :], 0.0),
             )
 
-        if k == 0:
+        if k == 1:
+            bias_sums[...] = jnp.zeros_like(bias_sums)
+        else:
             first_terms, second_terms, grad_own = node_terms()
             grads[2 * latent : 3 * latent, :] = grads[2 * latent : 3 * latent, :] + first_terms
+            grads[3 * latent : 4 * latent, :] = grads[3 * latent : 4 * latent, :] + second_terms
+
+        def folded(value):
+            pieces = [
+                value[:, at : at + LANES] for at in range(0, value.shape[1], LANES)
+            ]
+            return functools.reduce(lambda one, other: one + other, pieces)
+
+        def edge_back(cols):
+            both = nn(gm_part, onehot[slab : 2 * slab, cols])
+            edge_grad = both[0:latent]
+            hidden_grad = both[latent : 2 * latent] + both[2 * latent :]
+            if k == 0:
+                edge_grad = edge_grad + grad_edge[:, cols]
+                hidden_grad = hidden_grad + second_grad_edge[:, cols]
+            else:
+                grad_edge[:, cols] = edge_grad
+            pre_grad = hidden_grad * slopes[k, :, cols]
+            bias_sums[0] = bias_sums[0] + folded(pre_grad)
+            bias_sums[1] = bias_sums[1] + folded(edge_grad)
+            pre_grad = pre_grad.astype(BF16)
+            back_stack[0:latent, cols] = pre_grad
+            back_stack[latent : 2 * latent, cols] = pre_grad
+            back_stack[2 * latent : 3 * latent, cols] = edge_grad.astype(BF16)
+
+        chunks(slots, edge_back)
+
+        def weight_terms():
+            outer = nt(back_stack[latent : 3 * latent, :], hidden_in[k])
+            upper = outer[0:latent, 0:LANES]
+            lower = jnp.where(low_half, outer[0:latent, LANES:], outer[latent:, LANES:])
+            return upper, lower
+
+        if k == 0:
+            upper, lower = weight_terms()
+            grads[0:latent, :] = grads[0:latent, :] + upper
+            grads[latent : 2 * latent, :] = grads[latent : 2 * latent, :] + lower
+
+        if k == 0:
             grads[3 * latent : 4 * latent, :] = (
                 grads[3 * latent : 4 * latent, :]
-                + second_terms
                 + column_at(0, bias_sums[0])
                 + column_at(1, bias_sums[1])
             )
@@ -707,7 +706,6 @@
             node_grad[...] = (grad_own + total)[:, 0:latent]
             stores[2].start()
 
-    wait_bytes(sums_to.at[pl.ds(0, (n_plane - 1) * shard), :], recv_sem.at[11])
     wait_bytes(slab_land.at[pl.ds(0, slab - hits), :], send_sem.at[0])
     wait_bytes(rim_send, send_sem.at[1])
     wait_bytes(rim_near, send_sem.at[2])
@@ -725,6 +723,7 @@
     wait_bytes(plane_land, send_sem.at[11])
     for store in stores:
         store.wait()
+    wait_bytes(sums_to.at[pl.ds(0, (n_plane - 1) * shard), :], recv_sem.at[11])
 
 
 def deliver(*refs):
@@ -739,7 +738,7 @@
     stores = [
         pltpu.make_async_copy(held[at], targets[at], out_sem.at[at]) for at in range(8)
     ]
-    for load in loads:
+    for load in loads[::-1]:
         load.start()
     loads[3].wait()
     first[:, 0:LANES] = sums[0:latent, :]

time: 73 us -> 72.6 us (level)
  no operation moved by 1% of the time
where the time goes in v5:
time: 72.6 us; the launch traced here: 72.4 us
  Pallas kernels  71.1 us (98%)
  between operations  1.29 us (2%)
    pallas_call x1, Pallas kernels, body(): pl.pallas_call(functools.partial(kernel, n_phi, n_layer), out_shape=[*out...  69.2 us
    pallas_call x1, Pallas kernels, body(): pl.pallas_call(deliver, out_shape=outs, in_specs=[hbm] * 4, out_specs=[hb...  1.86 us

profile of v5, /device:TPU:1, one launch (start us, length us, event | category | flops | bytes accessed | tf_op | source)
XLA Modules:
  0.0 72.4 jit_solution(9107737785323648962)
XLA Ops:
  1.3 69.2 %shard_map.188 = (bf16[32,64]{1,0:T(8,128)(2,1)}, bf16[64,2048]{1,0:T(8,128)(2,1)}, f32[32,64]{1,0:T(8,128)}, f32[256,128]{1,0:T(8,128)}) custom-call(bf16[32,64]{1,0:T(8,128)(2,1)} %bitcast.7, bf16[64,2048]{1,0:T(8,128)(2,1)} %edges_in.1, s32[1,2048]{1,0:T(1,128)} %bitcast.8, s32[1,2048]{1,0:T(1,128)} %bitcast.9, s32[1,1]{1,0:T(1,128)S(6)} %copy.21.count_in, ...), custom_call_target="tpu_custom_call" | custom-call | tf_op jit(solution)/shard_map/pallas_call | solution.py:791
  70.5 1.9 %shard_map.189 = (bf16[32,64]{1,0:T(8,128)(2,1)}, bf16[64,2048]{1,0:T(8,128)(2,1)}, f32[32,64]{1,0:T(8,128)}, f32[64,192]{1,0:T(8,128)}, f32[64,64]{1,0:T(8,128)...) custom-call(bf16[32,64]{1,0:T(8,128)(2,1)} %get-tuple-element.20.refs_0_, ...), custom_call_target="tpu_custom_call" | custom-call | tf_op jit(solution)/shard_map/pallas_call | solution.py:841

commit v6 on v5

--- a/solution.py
+++ b/solution.py
@@ -14,7 +14,7 @@
 LANES = 128
 Y_LO = 2
 CORES = 2
-CHUNK = 1024
+CHUNK = 2048
 VMEM_BYTES = 64 * 1024 * 1024
 
 

time: 72.6 us -> 72.3 us (level)
  no operation moved by 1% of the time
where the time goes in v6:
time: 72.3 us; the launch traced here: 72.1 us
  Pallas kernels  70.8 us (98%)
  between operations  1.29 us (2%)
    pallas_call x1, Pallas kernels, body(): pl.pallas_call(functools.partial(kernel, n_phi, n_layer), out_shape=[*out...  69 us
    pallas_call x1, Pallas kernels, body(): pl.pallas_call(deliver, out_shape=outs, in_specs=[hbm] * 4, out_specs=[hb...  1.86 us

profile of v6, /device:TPU:1, one launch (start us, length us, event | category | flops | bytes accessed | tf_op | source)
XLA Modules:
  0.0 72.1 jit_solution(16746728942670416013)
XLA Ops:
  1.3 69.0 %shard_map.188 = (bf16[32,64]{1,0:T(8,128)(2,1)}, bf16[64,2048]{1,0:T(8,128)(2,1)}, f32[32,64]{1,0:T(8,128)}, f32[256,128]{1,0:T(8,128)}) custom-call(bf16[32,64]{1,0:T(8,128)(2,1)} %bitcast.7, bf16[64,2048]{1,0:T(8,128)(2,1)} %edges_in.1, s32[1,2048]{1,0:T(1,128)} %bitcast.8, s32[1,2048]{1,0:T(1,128)} %bitcast.9, s32[1,1]{1,0:T(1,128)S(6)} %copy.21.count_in, ...), custom_call_target="tpu_custom_call" | custom-call | tf_op jit(solution)/shard_map/pallas_call | solution.py:791
  70.3 1.9 %shard_map.189 = (bf16[32,64]{1,0:T(8,128)(2,1)}, bf16[64,2048]{1,0:T(8,128)(2,1)}, f32[32,64]{1,0:T(8,128)}, f32[64,192]{1,0:T(8,128)}, f32[64,64]{1,0:T(8,128)...) custom-call(bf16[32,64]{1,0:T(8,128)(2,1)} %get-tuple-element.20.refs_0_, ...), custom_call_target="tpu_custom_call" | custom-call | tf_op jit(solution)/shard_map/pallas_call | solution.py:841
